TPU v7x, 32 devices: a whole 2x2x4 slice. The times are simulated.
32 devices in a mesh: seq: 8 (over z, y), chan: 4 (over x, core).
Axes of the slice: x: 2, y: 2, z: 4, core: 2. Of those that a mesh axis runs over, the one named last changes fastest.
Arguments:
- tokens: bfloat16 [4096, 8192], P('seq', 'chan'), may hold values from -6 to 6
- norm_gain: float32 [8192], replicated, may hold values from 0.1 to 1.9
- w_in: bfloat16 [8192, 3, 4096], P('seq', None, 'chan'), may hold values from -0.0625 to 0.0625
- short_taps: float32 [3, 3, 4096], P(None, None, 'chan'), may hold values from -3.6 to 3.6
- medium_taps: float32 [128, 256], P(None, 'chan'), may hold values from -0.75 to 0.75
- skip_gain: float32 [4096], P('chan'), may hold values from 0.5 to 1.5
- w_out: bfloat16 [4096, 8192], P('chan'), may hold values from -0.09375 to 0.09375
Outputs:
- block_out: bfloat16 [4096, 8192], P('seq', 'chan')
All inputs are finite; a program needn't handle non-finite values.
Results may differ from a plain program's by a relative error of at most 0.019.
Values may be sent and summed in bfloat16 or wider, within the bound.
No kernel may reach another device: no remote copies, remote signals or barrier semaphores. Data moves between devices by JAX's collectives and lax.ppermute only.
A program may use at most 192 MiB of HBM per device.

v0:
```python
import jax
import jax.numpy as jnp
from jax import lax
from jax.experimental import pallas as pl
from jax.experimental.pallas import tpu as pltpu
from jax.sharding import PartitionSpec as P

TAPS = 128
GROUP = 16
EDGE = TAPS + 16
EPSILON = 1e-06
VMEM = 24 << 20
SHORT = pl.CostEstimate(flops=1, bytes_accessed=1, transcendentals=0)


def swapped(value, axis, bit):
    return lax.ppermute(value, axis, [(i, i ^ bit) for i in range(lax.axis_size(axis))])


def project(order, places, rows, sections, addend, near, ranks):
    depth = rows[0].shape[1]
    slabs = len(sections[0])
    branches, slab, width = sections[0][0].shape
    step = slabs * slab
    each = 2 * rows[0].shape[0] // (ranks * near)
    span = ranks * each
    count = near * span
    wide = branches * width
    flat = [value for section in sections for value in section]

    def kernel(order_ref, places_ref, *refs):
        gathered, total = refs[-2:]
        out_ref = refs[-3]
        for i in range(ranks):
            place = pl.multiple_of(places_ref[i] * each, each)
            for o in range(near):
                start = ((i // 2) * near + o) * each
                gathered[pl.ds(o * span + place, each)] = refs[i % 2][start : start + each]
        for i in range(len(flat)):
            place = pl.multiple_of(order_ref[i // slabs] * step + (i % slabs) * slab, slab)
            part = gathered[:, pl.ds(place, slab)]
            for b in range(branches):
                columns = slice(b * width, (b + 1) * width)
                value = jnp.dot(part, refs[2 + i][b], preferred_element_type=jnp.float32)
                if i == 0 and addend is not None:
                    value += refs[2 + len(flat)][:, columns].astype(jnp.float32)
                if i:
                    value += total[:, columns]
                if i < len(flat) - 1:
                    total[:, columns] = value
                else:
                    out_ref[:, columns] = value.astype(jnp.bfloat16)

    extra = [] if addend is None else [addend]
    smem = pl.BlockSpec(memory_space=pltpu.SMEM)
    vmem = pl.BlockSpec(memory_space=pltpu.VMEM)
    return pl.pallas_call(
        kernel,
        in_specs=[smem, smem] + [vmem] * (2 + len(flat) + len(extra)),
        out_specs=vmem,
        out_shape=jax.ShapeDtypeStruct((count, wide), jnp.bfloat16),
        scratch_shapes=[
            pltpu.VMEM((count, depth), jnp.bfloat16),
            pltpu.VMEM((count, wide), jnp.float32),
        ],
        compiler_params=pltpu.CompilerParams(vmem_limit_bytes=VMEM),
        cost_estimate=SHORT,
        name="project",
    )(order, places, *rows, *flat, *extra)


def gate(inputs, spans, row_count, short_taps, skip_gain, toeplitz):
    slots, _, wide = inputs[0].shape
    width = wide // 3
    filters = toeplitz.shape[1] // (2 * TAPS)
    reach = max(row_count, TAPS)

    def kernel(*refs):
        input_refs = refs[: len(inputs)]
        taps_ref, skip_ref, toeplitz_ref, out_ref, extended = refs[len(inputs) :]
        end = 0
        for ref, (first, last) in zip(input_refs, spans, strict=True):
            extended[end : end + last - first] = ref[0, first:last].astype(jnp.float32)
            end += last - first
        if row_count < TAPS:
            extended[end:] = jnp.zeros((TAPS - row_count, wide), jnp.float32)
        rows = TAPS + reach
        filtered = sum(
            taps_ref[lag : lag + 1] * extended[16 - lag : 16 - lag + rows] for lag in range(3)
        )
        product = filtered[:, width : 2 * width] * filtered[:, 2 * width :]
        product = product.astype(jnp.bfloat16)
        owner = lax.broadcasted_iota(jnp.int32, (2 * TAPS, width), 1) // GROUP
        for start in range(0, row_count, TAPS):
            start = min(start, reach - TAPS)
            size = min(TAPS, row_count)
            window = product[start : start + 2 * TAPS]
            spread = jnp.concatenate(
                [jnp.where(owner == f, window, jnp.zeros_like(window)) for f in range(filters)], 0
            )
            convolved = jnp.dot(toeplitz_ref[...], spread, preferred_element_type=jnp.float32)
            mixing = skip_ref[...] * window[TAPS:].astype(jnp.float32) + convolved
            queries = filtered[TAPS + start : 2 * TAPS + start, :width]
            out_ref[0, start : start + size] = (queries * mixing)[:size].astype(jnp.bfloat16)

    slot = lambda i: (i, 0, 0)
    fixed = lambda i: (0, 0)
    return pl.pallas_call(
        kernel,
        grid=(slots,),
        in_specs=[pl.BlockSpec((1,) + value.shape[1:], slot) for value in inputs]
        + [
            pl.BlockSpec((3, wide), fixed),
            pl.BlockSpec((1, width), fixed),
            pl.BlockSpec((TAPS, 2 * TAPS * filters), fixed),
        ],
        out_specs=pl.BlockSpec((1, row_count, width), slot),
        out_shape=jax.ShapeDtypeStruct((slots, row_count, width), jnp.bfloat16),
        scratch_shapes=[pltpu.VMEM((EDGE + reach, wide), jnp.float32)],
        compiler_params=pltpu.CompilerParams(vmem_limit_bytes=VMEM),
        cost_estimate=SHORT,
        name="gate",
    )(*inputs, short_taps, skip_gain, toeplitz)


def out_block(gating, w_out, block, count):
    rows, depth = gating.shape
    columns = w_out.shape[1] // count
    tile = min(columns, 512)
    steps = columns // tile

    def kernel(block_ref, gating_ref, w_ref, out_ref):
        out_ref[...] = jnp.dot(
            gating_ref[...], w_ref[...], preferred_element_type=jnp.float32
        ).astype(jnp.bfloat16)

    return pl.pallas_call(
        kernel,
        grid_spec=pltpu.PrefetchScalarGridSpec(
            num_scalar_prefetch=1,
            grid=(steps,),
            in_specs=[
                pl.BlockSpec((rows, depth), lambda i, b: (0, 0)),
                pl.BlockSpec((depth, tile), lambda i, b: (0, b[0] * steps + i)),
            ],
            out_specs=pl.BlockSpec((rows, tile), lambda i, b: (0, i)),
        ),
        out_shape=jax.ShapeDtypeStruct((rows, columns), jnp.bfloat16),
        compiler_params=pltpu.CompilerParams(vmem_limit_bytes=VMEM),
        cost_estimate=SHORT,
        name="out_block",
    )(block.reshape(1).astype(jnp.int32), gating, w_out)


def toeplitz_of(medium_taps):
    cube_shape = (TAPS, TAPS, 2 * TAPS)
    lagged = (
        lax.broadcasted_iota(jnp.int32, cube_shape, 1)
        + TAPS
        - lax.broadcasted_iota(jnp.int32, cube_shape, 2)
    )
    onehot = (lagged == lax.broadcasted_iota(jnp.int32, cube_shape, 0)).astype(jnp.bfloat16)
    return jnp.einsum("jg,jis->igs", medium_taps.astype(jnp.bfloat16), onehot)


def row_parts(row_count, ranks):
    unit = 16 * ranks
    units = row_count // unit
    low = max(1, units // 4)
    middle = (units - low) // 2
    sizes = [size * unit for size in (units - low - middle, middle, low) if size]
    ends = [row_count - sum(sizes[:i]) for i in range(len(sizes))]
    return [(end - size, end) for end, size in zip(ends, sizes, strict=True)]


def per_device(tokens, norm_gain, w_in, short_taps, medium_taps, skip_gain, w_out):
    seq, ranks = lax.axis_size("seq"), lax.axis_size("chan")
    here, column = lax.axis_index("seq"), lax.axis_index("chan")
    near = seq // 4
    odd, layer = here % 2, here // 2
    half, place = layer // near, layer % near
    row_count = tokens.shape[0]
    depth = norm_gain.shape[0]
    channels = w_in.shape[2]
    mine = channels // near
    pieces = max(1, mine // 256)
    width = mine // pieces
    parts = row_parts(row_count, ranks)
    slab = w_in.shape[0] // 2
    order = jnp.stack(
        [(place ^ o) * 2 + (odd ^ p) for o in range(near) for p in range(2)]
    ).astype(jnp.int32)
    places = jnp.stack([column ^ i for i in range(ranks)]).astype(jnp.int32)
    state = {}

    def cut(i, o, h):
        if h not in state:
            rows = jnp.transpose(w_in[h * slab : (h + 1) * slab], (1, 0, 2))
            state[h] = lax.optimization_barrier(rows)
        return lax.dynamic_slice_in_dim(state[h], (place ^ o) * mine + i * width, width, 2)

    def near_w(i, h):
        if i < pieces:
            for o in range(1, near):
                state["w", i, o, 0, h] = swapped(cut(i, o, h), "seq", 2 * o)

    def pair_own_w(i, h):
        if i < pieces:
            state["w", i, 0, 0, h] = own = cut(i, 0, h)
            state["w", i, 0, 1, h] = swapped(own, "seq", 1)

    def pair_near_w(i, h):
        if i < pieces:
            for o in range(1, near):
                state["w", i, o, 1, h] = swapped(state["w", i, o, 0, h], "seq", 1)

    def share():
        cuts = []
        for r in range(ranks):
            rows = []
            for first, last in parts:
                size = (last - first) // ranks
                rows.append(lax.dynamic_slice_in_dim(tokens, first + (column ^ r) * size, size, 0))
            cuts.append(jnp.concatenate(rows, 0))
        for r in range(ranks):
            state["shared", r] = cuts[r] if r == 0 else swapped(cuts[r], "chan", r)

    def norm(j):
        if j >= len(parts):
            return
        start = (row_count - parts[j][1]) // ranks
        size = (parts[j][1] - parts[j][0]) // ranks
        widened = [state["shared", r][start : start + size].astype(jnp.float32) for r in range(ranks)]
        square = sum(jnp.sum(piece * piece, axis=1, keepdims=True) for piece in widened)
        scale = lax.rsqrt(square / depth + EPSILON)
        gains = norm_gain.reshape(ranks, 1, depth // ranks)
        normed = jnp.stack(
            [
                (piece * scale * lax.dynamic_index_in_dim(gains, column ^ r, 0, False)).astype(jnp.bfloat16)
                for r, piece in enumerate(widened)
            ]
        )

        def of_half(which):
            chosen = [
                lax.dynamic_index_in_dim(normed, column ^ (which * (ranks // 2) + r), 0, False)
                for r in range(ranks // 2)
            ]
            return jnp.concatenate(chosen, 1)

        state["kept", j] = of_half(half)
        state["away", j] = of_half(1 - half)

    def cross(j):
        if j < len(parts):
            state["away", j] = swapped(state["away", j], "seq", 2 * near)

    def near_rows(kind, j):
        if j < len(parts):
            rows = state[kind, j]
            moved = [rows if o == 0 else swapped(rows, "seq", 2 * o) for o in range(near)]
            state[kind, j] = jnp.concatenate(moved, 0)

    def across(kind, j):
        if j < len(parts):
            rows = state[kind, j]
            moved = [rows if a == 0 else swapped(rows, "chan", 2 * a) for a in range(ranks // 2)]
            state[kind, j] = jnp.concatenate(moved, 0)

    def beside(kind, j):
        if j < len(parts):
            state["other", kind, j] = swapped(state[kind, j], "chan", 1)

    def multiplied(kind, i, j, addend):
        rows = [state[kind, j], state["other", kind, j]]
        sections = [[state["w", i, o, p, h] for h in range(2)] for o in range(near) for p in range(2)]
        return project(order, places, rows, sections, addend, near, ranks)

    def partial(i, j):
        if i < pieces and j < len(parts):
            state["partial", i, j] = multiplied("away", i, j, None)

    def send(i, j):
        if i < pieces and j < len(parts):
            state["moved", i, j] = swapped(state.pop(("partial", i, j)), "seq", 2 * near)

    def add(i, j):
        if i < pieces and j < len(parts):
            total = multiplied("kept", i, j, state.pop(("moved", i, j)))
            state["sum", i, j] = total.reshape(near, parts[j][1] - parts[j][0], 3 * width)

    def constants():
        short = lax.dynamic_slice_in_dim(short_taps, place * mine, mine, 2)
        skip = lax.dynamic_slice_in_dim(skip_gain, place * mine, mine, 0).reshape(1, mine)
        filters = medium_taps.shape[1] // near
        toeplitz = toeplitz_of(lax.dynamic_slice_in_dim(medium_taps, place * filters, filters, 1))
        some = filters // pieces
        for i in range(pieces):
            span = slice(i * width, (i + 1) * width)
            blocks = toeplitz[:, i * some : (i + 1) * some].reshape(TAPS, some * 2 * TAPS)
            state["constants", i, 0] = short[:, :, span].reshape(3, 3 * width)
            state["constants", i, 1] = skip[:, span]
            state["constants", i, 2] = blocks

    def step():
        held = lax.optimization_barrier(list(state.values()))
        state.update(zip(list(state), held, strict=True))

    share()
    pair_own_w(0, 0)
    near_w(0, 0)
    step()
    for j in range(len(parts)):
        norm(j)
    cross(0)
    pair_own_w(0, 1)
    near_w(0, 1)
    step()
    cross(1)
    constants()
    near_rows("away", 0)
    pair_near_w(0, 0)
    step()
    cross(2)
    across("away", 0)
    near_rows("away", 1)
    pair_near_w(0, 1)
    step()
    beside("away", 0)
    partial(0, 0)
    across("away", 1)
    near_rows("away", 2)
    near_w(1, 0)
    pair_own_w(1, 0)
    step()
    send(0, 0)
    beside("away", 1)
    partial(0, 1)
    across("away", 2)
    near_w(1, 1)
    pair_own_w(1, 1)
    step()
    send(0, 1)
    beside("away", 2)
    partial(0, 2)
    near_rows("kept", 0)
    pair_near_w(1, 0)
    step()
    send(0, 2)
    across("kept", 0)
    near_rows("kept", 1)
    pair_near_w(1, 1)
    step()
    partial(1, 0)
    send(1, 0)
    partial(1, 1)
    beside("kept", 0)
    across("kept", 1)
    near_rows("kept", 2)
    add(0, 0)
    step()
    send(1, 1)
    beside("kept", 1)
    across("kept", 2)
    add(1, 0)
    add(0, 1)
    partial(1, 2)
    step()
    send(1, 2)
    beside("kept", 2)

    far = [(2 * i + 1, 2 * (near + i)) for i in range(near)]

    def halo(i):
        edge = state["sum", i, 0][:, -EDGE:]
        edge = jnp.stack([lax.dynamic_index_in_dim(edge, place ^ o, 0, False) for o in range(near)])
        other = swapped(edge, "seq", 1)
        before = jnp.concatenate([lax.ppermute(edge[-1:], "seq", far), other[:-1]], 0)
        rows = jnp.where(odd == 1, other, before)
        return jnp.stack([lax.dynamic_index_in_dim(rows, place ^ o, 0, False) for o in range(near)])

    low = parts[-1][1] + EDGE

    def gated(i, inputs, spans, rows):
        return gate(inputs, spans, rows, *[state["constants", i, k] for k in range(3)])

    def joined(gates, rows):
        gating = jnp.zeros((rows, channels), jnp.bfloat16)
        for o in range(near):
            moved = [piece[o] if o == 0 else swapped(piece[o], "seq", 2 * o) for piece in gates]
            shares = jnp.concatenate(moved, 1)
            gating = lax.dynamic_update_slice(gating, shares, (0, (place ^ o) * mine))
        return gating

    def chip_sum(gating, a):
        target = column ^ (2 * a)
        other = swapped(out_block(gating, w_out, target ^ 1, ranks), "chan", 1)
        return out_block(gating, w_out, target, ranks).astype(jnp.float32) + other.astype(jnp.float32)

    def far_sums(gating):
        return [chip_sum(gating, a).astype(jnp.bfloat16) for a in range(1, ranks // 2)]

    def sent(sums):
        return [swapped(value, "chan", 2 * a) for a, value in enumerate(sums, 1)]

    def added(first, last, own, received):
        total = tokens[first:last].astype(jnp.float32) + own
        return (total + sum(value.astype(jnp.float32) for value in received)).astype(jnp.bfloat16)

    def all_gated(i):
        inputs = [state["sum", i, j] for j in reversed(range(len(parts) - 1))]
        return gated(i, inputs, [(0, value.shape[1]) for value in inputs], row_count - low)

    last = len(parts) - 1
    add(1, 1)
    upper = joined([all_gated(i) for i in range(pieces)], row_count - low)
    upper, *first_halos = lax.optimization_barrier([upper] + [halo(i) for i in range(pieces)])
    upper_sums = far_sums(upper)
    for i in range(pieces):
        if i:
            state["moved", i, last], upper_sums = lax.optimization_barrier((state["moved", i, last], upper_sums))
    upper_received = sent(upper_sums)
    lower = []
    for i in range(pieces):
        if last > 1 or i:
            add(i, last)
        lowest, next_up = state["sum", i, last], state["sum", i, last - 1]
        spans = [(0, EDGE), (0, lowest.shape[1]), (0, EDGE)]
        lower.append(gated(i, [first_halos[i], lowest, next_up], spans, low))
    lower = joined(lower, low)
    lower_sums = far_sums(lower)
    lower_sums, upper_received, lower = lax.optimization_barrier((lower_sums, upper_received, lower))
    lower_received = sent(lower_sums)
    upper = added(low, row_count, chip_sum(upper, 0), upper_received)
    lower = added(0, low, chip_sum(lower, 0), lower_received)
    return jnp.concatenate([lower, upper], 0)


def solution(mesh):
    in_specs = (
        P("seq", "chan"),
        P(),
        P("seq", None, "chan"),
        P(None, None, "chan"),
        P(None, "chan"),
        P("chan"),
        P("chan", None),
    )
    out_specs = P("seq", "chan")
    return jax.shard_map(
        per_device, mesh=mesh, in_specs=in_specs, out_specs=out_specs, check_vma=False
    )
```

profile of v0, /device:TPU:4, one launch (start us, length us, event | category | flops | bytes accessed | tf_op | source)
XLA Modules:
  0.0 417.7 jit_solution(5062526924809457737)
XLA Ops:
  0.0 6.8 %slice_bitcast_fusion = (bf16[3,512,1024]{2,1,0:T(8,128)(2,1)}, bf16[3,512,1024]{2,1,0:T(8,128)(2,1)}) fusion(bf16[1024,3,1024]{2,0,1:T(8,128)(2,1)} %param.9), kind=kLoop, calls=%fused_computation.3 | loop fusion | bytes 12582912 | tf_op jit(solution)/shard_map/transpose | solution.py:198
  22.9 4.1 fusion.2
  27.0 3.8 collective-permute-done.1
  32.3 7.0 %collective-permute-done.2 = bf16[128,2048]{1,0:T(8,128)(2,1)} collective-permute-done((bf16[128,2048]{1,0:T(8,128)(2,1)}, bf16[128,2048]{1,0:T(8,128)(2,1)}, u32[]{:S(2)}, u32[]{:S(2)}) %collective-permute-start.2) | collective-permute-done | bytes 524320 | tf_op jit(solution)/shard_map/ppermute | solution.py:17
  55.3 12.9 %collective-permute-done.7.refs_7_ = bf16[3,512,256]{2,1,0:T(8,128)(2,1)} collective-permute-done((bf16[3,512,256]{2,1,0:T(8,128)(2,1)S(1)}, bf16[3,512,256]{2,1,0:T(8,128)(2,1)}, u32[]{:S(2)}, u32[]{:S(2)}) %collective-permute-start.7) | collective-permute-done | bytes 786464 | tf_op jit(solution)/shard_map/ppermute | solution.py:17
  78.7 5.6 %collective-permute-done.8 = bf16[48,4096]{1,0:T(8,128)(2,1)} collective-permute-done((bf16[48,4096]{1,0:T(8,128)(2,1)}, bf16[48,4096]{1,0:T(8,128)(2,1)}, u32[]{:S(2)}, u32[]{:S(2)}) %collective-permute-start.8) | collective-permute-done | bytes 393248 | tf_op jit(solution)/shard_map/ppermute | solution.py:17
  85.5 10.5 %collective-permute-done.9 = bf16[48,4096]{1,0:T(8,128)(2,1)S(1)} collective-permute-done((bf16[48,4096]{1,0:T(8,128)(2,1)}, bf16[48,4096]{1,0:T(8,128)(2,1)S(1)}, u32[]{:S(2)}, u32[]{:S(2)}) %collective-permute-start.9) | collective-permute-done | bytes 393248 | tf_op jit(solution)/shard_map/ppermute | solution.py:17
  101.2 11.0 %collective-permute-done.12 = bf16[48,4096]{1,0:T(8,128)(2,1)S(1)} collective-permute-done((bf16[48,4096]{1,0:T(8,128)(2,1)S(1)}, bf16[48,4096]{1,0:T(8,128)(2,1)S(1)}, u32[]{:S(2)}, u32[]{:S(2)}) %collective-permute-start.12) | collective-permute-done | bytes 393248 | tf_op jit(solution)/shard_map/ppermute | solution.py:17
  122.8 5.1 %collective-permute-done.16 = bf16[32,4096]{1,0:T(8,128)(2,1)S(1)} collective-permute-done((bf16[32,4096]{1,0:T(8,128)(2,1)}, bf16[32,4096]{1,0:T(8,128)(2,1)S(1)}, u32[]{:S(2)}, u32[]{:S(2)}) %collective-permute-start.16) | collective-permute-done | bytes 262176 | tf_op jit(solution)/shard_map/ppermute | solution.py:17
  128.9 8.6 %collective-permute-done.15 = bf16[96,4096]{1,0:T(8,128)(2,1)} collective-permute-done((bf16[96,4096]{1,0:T(8,128)(2,1)}, bf16[96,4096]{1,0:T(8,128)(2,1)}, u32[]{:S(2)}, u32[]{:S(2)}) %collective-permute-start.15) | collective-permute-done | bytes 786464 | tf_op jit(solution)/shard_map/ppermute | solution.py:17
  139.1 5.1 %project.12 = bf16[384,768]{1,0:T(8,128)(2,1)S(1)} custom-call(s32[4]{0:T(128)S(1)} %get-tuple-element.611.order_ref, s32[4]{0:T(128)S(1)} %get-tuple-element.612.places_ref, bf16[192,4096]{1,0:T(8,128)(2,1)} %pad_maximum_fusion.1.refs_0_, bf16[192,4096]{1,0:T(8,128)(2,1)} %collective-permute-done.17.refs_1_, ...), custom_call_target="tpu_custom_call" | custom-call | flops 1 | bytes 1 | tf_op jit(solution)/shard_map/project/pallas_call | solution.py:57
  149.4 9.2 %collective-permute-done.20 = bf16[64,4096]{1,0:T(8,128)(2,1)S(1)} collective-permute-done((bf16[64,4096]{1,0:T(8,128)(2,1)S(1)}, bf16[64,4096]{1,0:T(8,128)(2,1)S(1)}, u32[]{:S(2)}, u32[]{:S(2)}) %collective-permute-start.20) | collective-permute-done | bytes 524320 | tf_op jit(solution)/shard_map/ppermute | solution.py:17
  158.7 4.4 %project.13 = bf16[384,768]{1,0:T(8,128)(2,1)S(1)} custom-call(s32[4]{0:T(128)S(1)} %get-tuple-element.611.order_ref, s32[4]{0:T(128)S(1)} %get-tuple-element.612.places_ref, bf16[192,4096]{1,0:T(8,128)(2,1)S(1)} %pad_maximum_fusion.2.refs_0_, bf16[192,4096]{1,0:T(8,128)(2,1)S(1)} %collective-permute-done.22.refs_1_, ...), custom_call_target="tpu_custom_call" | custom-call | flops 1 | bytes 1 | tf_op jit(solution)/shard_map/project/pallas_call | solution.py:57
  163.1 14.3 %collective-permute-done.21.refs_10_ = bf16[384,768]{1,0:T(8,128)(2,1)S(1)} collective-permute-done((bf16[384,768]{1,0:T(8,128)(2,1)S(1)}, bf16[384,768]{1,0:T(8,128)(2,1)S(1)}, u32[]{:S(2)}, u32[]{:S(2)}) %collective-permute-start.21) | collective-permute-done | bytes 589856 | tf_op jit(solution)/shard_map/ppermute | solution.py:17
  181.8 16.0 %collective-permute-done.25 = bf16[48,4096]{1,0:T(8,128)(2,1)S(1)} collective-permute-done((bf16[48,4096]{1,0:T(8,128)(2,1)S(1)}, bf16[48,4096]{1,0:T(8,128)(2,1)S(1)}, u32[]{:S(2)}, u32[]{:S(2)}) %collective-permute-start.25) | collective-permute-done | bytes 393248 | tf_op jit(solution)/shard_map/ppermute | solution.py:17
  197.9 3.7 project.14
  201.6 8.7 %collective-permute-done.26.refs_10_ = bf16[384,768]{1,0:T(8,128)(2,1)S(1)} collective-permute-done((bf16[384,768]{1,0:T(8,128)(2,1)S(1)}, bf16[384,768]{1,0:T(8,128)(2,1)S(1)}, u32[]{:S(2)}, u32[]{:S(2)}) %collective-permute-start.26) | collective-permute-done | bytes 589856 | tf_op jit(solution)/shard_map/ppermute | solution.py:17
  214.5 11.4 %collective-permute-done.30 = bf16[48,4096]{1,0:T(8,128)(2,1)S(1)} collective-permute-done((bf16[48,4096]{1,0:T(8,128)(2,1)S(1)}, bf16[48,4096]{1,0:T(8,128)(2,1)S(1)}, u32[]{:S(2)}, u32[]{:S(2)}) %collective-permute-start.30) | collective-permute-done | bytes 393248 | tf_op jit(solution)/shard_map/ppermute | solution.py:17
  233.6 4.7 %project.15 = bf16[384,768]{1,0:T(8,128)(2,1)S(1)} custom-call(s32[4]{0:T(128)S(1)} %get-tuple-element.611.order_ref, s32[4]{0:T(128)S(1)} %get-tuple-element.612.places_ref, bf16[192,4096]{1,0:T(8,128)(2,1)} %pad_maximum_fusion.1.refs_0_, bf16[192,4096]{1,0:T(8,128)(2,1)} %collective-permute-done.17.refs_1_, ...), custom_call_target="tpu_custom_call" | custom-call | flops 1 | bytes 1 | tf_op jit(solution)/shard_map/project/pallas_call | solution.py:57
  240.5 4.2 %project.16 = bf16[384,768]{1,0:T(8,128)(2,1)} custom-call(s32[4]{0:T(128)S(1)} %get-tuple-element.611.order_ref, s32[4]{0:T(128)S(1)} %get-tuple-element.612.places_ref, bf16[192,4096]{1,0:T(8,128)(2,1)S(1)} %pad_maximum_fusion.2.refs_0_, bf16[192,4096]{1,0:T(8,128)(2,1)S(1)} %collective-permute-done.22.refs_1_, ...), custom_call_target="tpu_custom_call" | custom-call | flops 1 | bytes 1 | tf_op jit(solution)/shard_map/project/pallas_call | solution.py:57
  245.6 6.6 %collective-permute-done.33 = bf16[96,4096]{1,0:T(8,128)(2,1)S(1)} collective-permute-done((bf16[96,4096]{1,0:T(8,128)(2,1)S(1)}, bf16[96,4096]{1,0:T(8,128)(2,1)S(1)}, u32[]{:S(2)}, u32[]{:S(2)}) %collective-permute-start.33) | collective-permute-done | bytes 786464 | tf_op jit(solution)/shard_map/ppermute | solution.py:17
  253.5 4.5 %project.17 = bf16[384,768]{1,0:T(8,128)(2,1)S(1)} custom-call(s32[4]{0:T(128)S(1)} %get-tuple-element.611.order_ref, s32[4]{0:T(128)S(1)} %get-tuple-element.612.places_ref, bf16[192,4096]{1,0:T(8,128)(2,1)S(1)} %pad_maximum_fusion.3.refs_0_, bf16[192,4096]{1,0:T(8,128)(2,1)S(1)} %collective-permute-done.36.refs_1_, ...), custom_call_target="tpu_custom_call" | custom-call | flops 1 | bytes 1 | tf_op jit(solution)/shard_map/project/pallas_call | solution.py:57
  258.9 8.4 %collective-permute-done.35.refs_10_ = bf16[384,768]{1,0:T(8,128)(2,1)S(1)} collective-permute-done((bf16[384,768]{1,0:T(8,128)(2,1)S(1)}, bf16[384,768]{1,0:T(8,128)(2,1)S(1)}, u32[]{:S(2)}, u32[]{:S(2)}) %collective-permute-start.35) | collective-permute-done | bytes 589856 | tf_op jit(solution)/shard_map/ppermute | solution.py:17
  286.8 5.1 %project.19 = bf16[384,768]{1,0:T(8,128)(2,1)S(1)} custom-call(s32[4]{0:T(128)S(1)} %get-tuple-element.611.order_ref, s32[4]{0:T(128)S(1)} %get-tuple-element.612.places_ref, bf16[192,4096]{1,0:T(8,128)(2,1)} %pad_maximum_fusion.4.refs_0_, bf16[192,4096]{1,0:T(8,128)(2,1)} %collective-permute-done.39.refs_1_, ...), custom_call_target="tpu_custom_call" | custom-call | flops 1 | bytes 1 | tf_op jit(solution)/shard_map/project/pallas_call | solution.py:57
  291.9 5.2 %collective-permute-done.38.refs_10_ = bf16[384,768]{1,0:T(8,128)(2,1)} collective-permute-done((bf16[384,768]{1,0:T(8,128)(2,1)}, bf16[384,768]{1,0:T(8,128)(2,1)}, u32[]{:S(2)}, u32[]{:S(2)}) %collective-permute-start.38) | collective-permute-done | bytes 589856 | tf_op jit(solution)/shard_map/ppermute | solution.py:17
  300.9 5.0 %project.21 = bf16[384,768]{1,0:T(8,128)(2,1)S(1)} custom-call(s32[4]{0:T(128)S(1)} %get-tuple-element.611.order_ref, s32[4]{0:T(128)S(1)} %get-tuple-element.612.places_ref, bf16[192,4096]{1,0:T(8,128)(2,1)} %pad_maximum_fusion.4.refs_0_, bf16[192,4096]{1,0:T(8,128)(2,1)} %collective-permute-done.39.refs_1_, ...), custom_call_target="tpu_custom_call" | custom-call | flops 1 | bytes 1 | tf_op jit(solution)/shard_map/project/pallas_call | solution.py:57
  318.0 5.3 %collective-permute-done.42 = bf16[2,144,768]{2,1,0:T(8,128)(2,1)S(1)} collective-permute-done((bf16[2,144,768]{2,1,0:T(8,128)(2,1)S(1)}, bf16[2,144,768]{2,1,0:T(8,128)(2,1)S(1)}, u32[]{:S(2)}, u32[]{:S(2)}) %collective-permute-start.42) | collective-permute-done | bytes 442400 | tf_op jit(solution)/shard_map/ppermute | solution.py:17
  326.0 4.1 collective-permute-start.47
  341.7 6.8 %collective-permute-done.47.refs_10_ = bf16[256,768]{1,0:T(8,128)(2,1)S(1)} collective-permute-done((bf16[256,768]{1,0:T(8,128)(2,1)}, bf16[256,768]{1,0:T(8,128)(2,1)S(1)}, u32[]{:S(2)}, u32[]{:S(2)}) %collective-permute-start.47) | collective-permute-done | bytes 393248 | tf_op jit(solution)/shard_map/ppermute | solution.py:17
  354.5 4.5 %collective-permute-done.50 = bf16[272,256]{1,0:T(8,128)(2,1)S(1)} collective-permute-done((bf16[272,256]{1,0:T(8,128)(2,1)S(1)}, bf16[272,256]{1,0:T(8,128)(2,1)S(1)}, u32[]{:S(2)}, u32[]{:S(2)}) %collective-permute-start.50) | collective-permute-done | bytes 139296 | tf_op jit(solution)/shard_map/ppermute | solution.py:17
  367.8 17.7 %collective-permute-done.52 = bf16[240,2048]{1,0:T(8,128)(2,1)S(1)} collective-permute-done((bf16[240,2048]{1,0:T(8,128)(2,1)S(1)}, bf16[240,2048]{1,0:T(8,128)(2,1)S(1)}, u32[]{:S(2)}, u32[]{:S(2)}) %collective-permute-start.52) | collective-permute-done | bytes 983072 | tf_op jit(solution)/shard_map/ppermute | solution.py:17
  394.4 20.5 %collective-permute-done.54 = bf16[272,2048]{1,0:T(8,128)(2,1)S(1)} collective-permute-done((bf16[272,2048]{1,0:T(8,128)(2,1)S(1)}, bf16[272,2048]{1,0:T(8,128)(2,1)S(1)}, u32[]{:S(2)}, u32[]{:S(2)}) %collective-permute-start.54) | collective-permute-done | bytes 1114144 | tf_op jit(solution)/shard_map/ppermute | solution.py:17
  (318 shorter events, 165.2 us)
Async XLA Ops:
  9.2 30.5 %collective-permute-start.3 = (bf16[3,512,256]{2,1,0:T(8,128)(2,1)S(1)}, bf16[3,512,256]{2,1,0:T(8,128)(2,1)S(1)}, u32[]{:S(2)}, u32[]{:S(2)}) collective-permute-start(bf16[3,512,256]{2,1,0:T(8,128)(2,1)S(1)} %get-tuple-element.508.refs_2_), channel_id=1, source_target_pairs={{0,4},{4,0},{8,12},{12,8},{16,20},{20,16},{24,28},{28,24},{1,5},{5... | collective-permute-start | bytes 2359304 | tf_op jit(solution)/shard_map/ppermute | solution.py:17
  9.2 30.5 %collective-permute-start.4 = (bf16[3,512,256]{2,1,0:T(8,128)(2,1)}, bf16[3,512,256]{2,1,0:T(8,128)(2,1)S(1)}, u32[]{:S(2)}, u32[]{:S(2)}) collective-permute-start(bf16[3,512,256]{2,1,0:T(8,128)(2,1)} %get-tuple-element.541), channel_id=1, source_target_pairs={{0,8},{4,12},{8,0},{12,4},{16,24},{20,28},{24,16},{28,20},{1,9},{5... | collective-permute-start | bytes 2359304 | tf_op jit(solution)/shard_map/ppermute | solution.py:17
  17.9 21.3 %collective-permute-start.2 = (bf16[128,2048]{1,0:T(8,128)(2,1)}, bf16[128,2048]{1,0:T(8,128)(2,1)}, u32[]{:S(2)}, u32[]{:S(2)}) collective-permute-start(bf16[128,2048]{1,0:T(8,128)(2,1)} %pad_maximum_fusion.16), channel_id=1, source_target_pairs={{0,3},{1,2},{2,1},{3,0},{4,7},{5,6},{6,5},{7,4},{8,11},{9,10},{10,... | collective-permute-start | bytes 1572872 | tf_op jit(solution)/shard_map/ppermute | solution.py:17
  18.8 21.0 %collective-permute-start = (bf16[128,2048]{1,0:T(8,128)(2,1)}, bf16[128,2048]{1,0:T(8,128)(2,1)}, u32[]{:S(2)}, u32[]{:S(2)}) collective-permute-start(bf16[128,2048]{1,0:T(8,128)(2,1)} %pad_maximum_fusion.14), channel_id=1, source_target_pairs={{0,1},{1,0},{2,3},{3,2},{4,5},{5,4},{6,7},{7,6},{8,9},{9,8},{10,11... | collective-permute-start | bytes 1572872 | tf_op jit(solution)/shard_map/ppermute | solution.py:17
  30.8 23.6 %collective-permute-start.6 = (bf16[3,512,256]{2,1,0:T(8,128)(2,1)S(1)}, bf16[3,512,256]{2,1,0:T(8,128)(2,1)S(1)}, u32[]{:S(2)}, u32[]{:S(2)}) collective-permute-start(bf16[3,512,256]{2,1,0:T(8,128)(2,1)S(1)} %get-tuple-element.509.refs_3_), channel_id=1, source_target_pairs={{0,4},{4,0},{8,12},{12,8},{16,20},{20,16},{24,28},{28,24},{1,5},{5... | collective-permute-start | bytes 2359304 | tf_op jit(solution)/shard_map/ppermute | solution.py:17
  39.3 28.9 %collective-permute-start.7 = (bf16[3,512,256]{2,1,0:T(8,128)(2,1)S(1)}, bf16[3,512,256]{2,1,0:T(8,128)(2,1)}, u32[]{:S(2)}, u32[]{:S(2)}) collective-permute-start(bf16[3,512,256]{2,1,0:T(8,128)(2,1)S(1)} %copy-done.56), channel_id=1, source_target_pairs={{0,8},{4,12},{8,0},{12,4},{16,24},{20,28},{24,16},{28,20},{1,9},{5... | collective-permute-start | bytes 2359304 | tf_op jit(solution)/shard_map/ppermute | solution.py:17
  48.6 19.6 %collective-permute-start.5 = (bf16[48,4096]{1,0:T(8,128)(2,1)S(1)}, bf16[48,4096]{1,0:T(8,128)(2,1)}, u32[]{:S(2)}, u32[]{:S(2)}) collective-permute-start(bf16[48,4096]{1,0:T(8,128)(2,1)S(1)} %pad_maximum_fusion.25), channel_id=1, source_target_pairs={{0,16},{4,20},{8,24},{12,28},{16,0},{20,4},{24,8},{28,12},{1,17},{... | collective-permute-start | bytes 1179656 | tf_op jit(solution)/shard_map/ppermute | solution.py:17
  73.7 22.2 %collective-permute-start.10 = (bf16[3,512,256]{2,1,0:T(8,128)(2,1)S(1)}, bf16[3,512,256]{2,1,0:T(8,128)(2,1)S(1)}, u32[]{:S(2)}, u32[]{:S(2)}) collective-permute-start(bf16[3,512,256]{2,1,0:T(8,128)(2,1)S(1)} %collective-permute-done.4.refs_6_), channel_id=1, source_target_pairs={{0,4},{4,0},{8,12},{12,8},{16,20},{20,16},{24,28},{28,24},{1,5},{5... | collective-permute-start | bytes 2359304 | tf_op jit(solution)/shard_map/ppermute | solution.py:17
  75.4 20.6 %collective-permute-start.9 = (bf16[48,4096]{1,0:T(8,128)(2,1)}, bf16[48,4096]{1,0:T(8,128)(2,1)S(1)}, u32[]{:S(2)}, u32[]{:S(2)}) collective-permute-start(bf16[48,4096]{1,0:T(8,128)(2,1)} %pad_maximum_fusion.27), channel_id=1, source_target_pairs={{0,16},{4,20},{8,24},{12,28},{16,0},{20,4},{24,8},{28,12},{1,17},{... | collective-permute-start | bytes 1179656 | tf_op jit(solution)/shard_map/ppermute | solution.py:17
  117.2 21.8 %collective-permute-start.17 = (bf16[192,4096]{1,0:T(8,128)(2,1)}, bf16[192,4096]{1,0:T(8,128)(2,1)}, u32[]{:S(2)}, u32[]{:S(2)}) collective-permute-start(bf16[192,4096]{1,0:T(8,128)(2,1)} %pad_maximum_fusion.1.refs_0_), channel_id=1, source_target_pairs={{0,1},{1,0},{2,3},{3,2},{4,5},{5,4},{6,7},{7,6},{8,9},{9,8},{10,11... | collective-permute-start | bytes 4718600 | tf_op jit(solution)/shard_map/ppermute | solution.py:17
  117.2 20.3 %collective-permute-start.15 = (bf16[96,4096]{1,0:T(8,128)(2,1)}, bf16[96,4096]{1,0:T(8,128)(2,1)}, u32[]{:S(2)}, u32[]{:S(2)}) collective-permute-start(bf16[96,4096]{1,0:T(8,128)(2,1)} %pad_maximum_fusion.10), channel_id=1, source_target_pairs={{0,2},{1,3},{2,0},{3,1},{4,6},{5,7},{6,4},{7,5},{8,10},{9,11},{10,... | collective-permute-start | bytes 2359304 | tf_op jit(solution)/shard_map/ppermute | solution.py:17
  121.9 22.3 %collective-permute-start.18 = (bf16[3,512,256]{2,1,0:T(8,128)(2,1)S(1)}, bf16[3,512,256]{2,1,0:T(8,128)(2,1)S(1)}, u32[]{:S(2)}, u32[]{:S(2)}) collective-permute-start(bf16[3,512,256]{2,1,0:T(8,128)(2,1)S(1)} %get-tuple-element.538), channel_id=1, source_target_pairs={{0,8},{4,12},{8,0},{12,4},{16,24},{20,28},{24,16},{28,20},{1,9},{5... | collective-permute-start | bytes 2359304 | tf_op jit(solution)/shard_map/ppermute | solution.py:17
  122.2 22.0 %collective-permute-start.19 = (bf16[3,512,256]{2,1,0:T(8,128)(2,1)S(1)}, bf16[3,512,256]{2,1,0:T(8,128)(2,1)S(1)}, u32[]{:S(2)}, u32[]{:S(2)}) collective-permute-start(bf16[3,512,256]{2,1,0:T(8,128)(2,1)S(1)} %get-tuple-element.493.refs_2_), channel_id=1, source_target_pairs={{0,4},{4,0},{8,12},{12,8},{16,20},{20,16},{24,28},{28,24},{1,5},{5... | collective-permute-start | bytes 2359304 | tf_op jit(solution)/shard_map/ppermute | solution.py:17
  145.9 32.3 %collective-permute-start.23 = (bf16[3,512,256]{2,1,0:T(8,128)(2,1)S(1)}, bf16[3,512,256]{2,1,0:T(8,128)(2,1)S(1)}, u32[]{:S(2)}, u32[]{:S(2)}) collective-permute-start(bf16[3,512,256]{2,1,0:T(8,128)(2,1)S(1)} %get-tuple-element.536), channel_id=1, source_target_pairs={{0,8},{4,12},{8,0},{12,4},{16,24},{20,28},{24,16},{28,20},{1,9},{5... | collective-permute-start | bytes 2359304 | tf_op jit(solution)/shard_map/ppermute | solution.py:17
  147.7 30.5 %collective-permute-start.24 = (bf16[3,512,256]{2,1,0:T(8,128)(2,1)S(1)}, bf16[3,512,256]{2,1,0:T(8,128)(2,1)S(1)}, u32[]{:S(2)}, u32[]{:S(2)}) collective-permute-start(bf16[3,512,256]{2,1,0:T(8,128)(2,1)S(1)} %get-tuple-element.494.refs_3_), channel_id=1, source_target_pairs={{0,4},{4,0},{8,12},{12,8},{16,20},{20,16},{24,28},{28,24},{1,5},{5... | collective-permute-start | bytes 2359304 | tf_op jit(solution)/shard_map/ppermute | solution.py:17
  148.2 29.3 %collective-permute-start.21 = (bf16[384,768]{1,0:T(8,128)(2,1)S(1)}, bf16[384,768]{1,0:T(8,128)(2,1)S(1)}, u32[]{:S(2)}, u32[]{:S(2)}) collective-permute-start(bf16[384,768]{1,0:T(8,128)(2,1)S(1)} %project.12), channel_id=1, source_target_pairs={{0,16},{4,20},{8,24},{12,28},{16,0},{20,4},{24,8},{28,12},{1,17},{... | collective-permute-start | bytes 1769480 | tf_op jit(solution)/shard_map/ppermute | solution.py:17
  178.2 19.6 %collective-permute-start.27 = (bf16[128,4096]{1,0:T(8,128)(2,1)S(1)}, bf16[128,4096]{1,0:T(8,128)(2,1)S(1)}, u32[]{:S(2)}, u32[]{:S(2)}) collective-permute-start(bf16[128,4096]{1,0:T(8,128)(2,1)S(1)} %pad_maximum_fusion.5.refs_0_), channel_id=1, source_target_pairs={{0,1},{1,0},{2,3},{3,2},{4,5},{5,4},{6,7},{7,6},{8,9},{9,8},{10,11... | collective-permute-start | bytes 3145736 | tf_op jit(solution)/shard_map/ppermute | solution.py:17
  178.3 19.5 %collective-permute-start.25 = (bf16[48,4096]{1,0:T(8,128)(2,1)S(1)}, bf16[48,4096]{1,0:T(8,128)(2,1)S(1)}, u32[]{:S(2)}, u32[]{:S(2)}) collective-permute-start(bf16[48,4096]{1,0:T(8,128)(2,1)S(1)} %copy-done.55), channel_id=1, source_target_pairs={{0,8},{4,12},{8,0},{12,4},{16,24},{20,28},{24,16},{28,20},{1,9},{5... | collective-permute-start | bytes 1179656 | tf_op jit(solution)/shard_map/ppermute | solution.py:17
  181.0 29.2 %collective-permute-start.28 = (bf16[3,512,256]{2,1,0:T(8,128)(2,1)S(1)}, bf16[3,512,256]{2,1,0:T(8,128)(2,1)S(1)}, u32[]{:S(2)}, u32[]{:S(2)}) collective-permute-start(bf16[3,512,256]{2,1,0:T(8,128)(2,1)S(1)} %collective-permute-done.18.refs_6_), channel_id=1, source_target_pairs={{0,4},{4,0},{8,12},{12,8},{16,20},{20,16},{24,28},{28,24},{1,5},{5... | collective-permute-start | bytes 2359304 | tf_op jit(solution)/shard_map/ppermute | solution.py:17
  181.5 28.7 %collective-permute-start.26 = (bf16[384,768]{1,0:T(8,128)(2,1)S(1)}, bf16[384,768]{1,0:T(8,128)(2,1)S(1)}, u32[]{:S(2)}, u32[]{:S(2)}) collective-permute-start(bf16[384,768]{1,0:T(8,128)(2,1)S(1)} %project.13), channel_id=1, source_target_pairs={{0,16},{4,20},{8,24},{12,28},{16,0},{20,4},{24,8},{28,12},{1,17},{... | collective-permute-start | bytes 1769480 | tf_op jit(solution)/shard_map/ppermute | solution.py:17
  211.1 21.2 %collective-permute-start.32 = (bf16[3,512,256]{2,1,0:T(8,128)(2,1)S(1)}, bf16[3,512,256]{2,1,0:T(8,128)(2,1)S(1)}, u32[]{:S(2)}, u32[]{:S(2)}) collective-permute-start(bf16[3,512,256]{2,1,0:T(8,128)(2,1)S(1)} %collective-permute-done.23.refs_7_), channel_id=1, source_target_pairs={{0,4},{4,0},{8,12},{12,8},{16,20},{20,16},{24,28},{28,24},{1,5},{5... | collective-permute-start | bytes 2359304 | tf_op jit(solution)/shard_map/ppermute | solution.py:17
  212.6 18.9 %collective-permute-start.31 = (bf16[256,768]{1,0:T(8,128)(2,1)S(1)}, bf16[256,768]{1,0:T(8,128)(2,1)S(1)}, u32[]{:S(2)}, u32[]{:S(2)}) collective-permute-start(bf16[256,768]{1,0:T(8,128)(2,1)S(1)} %project.14), channel_id=1, source_target_pairs={{0,16},{4,20},{8,24},{12,28},{16,0},{20,4},{24,8},{28,12},{1,17},{... | collective-permute-start | bytes 1179656 | tf_op jit(solution)/shard_map/ppermute | solution.py:17
  232.2 21.3 %collective-permute-start.36 = (bf16[192,4096]{1,0:T(8,128)(2,1)S(1)}, bf16[192,4096]{1,0:T(8,128)(2,1)S(1)}, u32[]{:S(2)}, u32[]{:S(2)}) collective-permute-start(bf16[192,4096]{1,0:T(8,128)(2,1)S(1)} %pad_maximum_fusion.3.refs_0_), channel_id=1, source_target_pairs={{0,1},{1,0},{2,3},{3,2},{4,5},{5,4},{6,7},{7,6},{8,9},{9,8},{10,11... | collective-permute-start | bytes 4718600 | tf_op jit(solution)/shard_map/ppermute | solution.py:17
  232.2 20.0 %collective-permute-start.33 = (bf16[96,4096]{1,0:T(8,128)(2,1)S(1)}, bf16[96,4096]{1,0:T(8,128)(2,1)S(1)}, u32[]{:S(2)}, u32[]{:S(2)}) collective-permute-start(bf16[96,4096]{1,0:T(8,128)(2,1)S(1)} %pad_maximum_fusion.12), channel_id=1, source_target_pairs={{0,2},{1,3},{2,0},{3,1},{4,6},{5,7},{6,4},{7,5},{8,10},{9,11},{10,... | collective-permute-start | bytes 2359304 | tf_op jit(solution)/shard_map/ppermute | solution.py:17
  238.4 29.0 %collective-permute-start.35 = (bf16[384,768]{1,0:T(8,128)(2,1)S(1)}, bf16[384,768]{1,0:T(8,128)(2,1)S(1)}, u32[]{:S(2)}, u32[]{:S(2)}) collective-permute-start(bf16[384,768]{1,0:T(8,128)(2,1)S(1)} %project.15), channel_id=1, source_target_pairs={{0,16},{4,20},{8,24},{12,28},{16,0},{20,4},{24,8},{28,12},{1,17},{... | collective-permute-start | bytes 1769480 | tf_op jit(solution)/shard_map/ppermute | solution.py:17
  268.9 28.1 %collective-permute-start.38 = (bf16[384,768]{1,0:T(8,128)(2,1)}, bf16[384,768]{1,0:T(8,128)(2,1)}, u32[]{:S(2)}, u32[]{:S(2)}) collective-permute-start(bf16[384,768]{1,0:T(8,128)(2,1)} %project.16), channel_id=1, source_target_pairs={{0,16},{4,20},{8,24},{12,28},{16,0},{20,4},{24,8},{28,12},{1,17},{... | collective-permute-start | bytes 1769480 | tf_op jit(solution)/shard_map/ppermute | solution.py:17
  297.1 20.8 %collective-permute-start.45 = (bf16[1,144,768]{2,1,0:T(8,128)(2,1)S(1)}, bf16[1,144,768]{2,1,0:T(8,128)(2,1)S(1)}, u32[]{:S(2)}, u32[]{:S(2)}) collective-permute-start(bf16[1,144,768]{2,1,0:T(8,128)(2,1)S(1)} %get-tuple-element.580), channel_id=1, source_target_pairs={{4,16},{12,24},{5,17},{13,25},{6,18},{14,26},{7,19},{15,27}} | collective-permute-start | bytes 663560 | tf_op jit(solution)/shard_map/ppermute | solution.py:378
  298.6 19.2 %collective-permute-start.44 = (bf16[2,144,768]{2,1,0:T(8,128)(2,1)S(1)}, bf16[2,144,768]{2,1,0:T(8,128)(2,1)S(1)}, u32[]{:S(2)}, u32[]{:S(2)}) collective-permute-start(bf16[2,144,768]{2,1,0:T(8,128)(2,1)S(1)} %pad_maximum_fusion.22), channel_id=1, source_target_pairs={{0,4},{4,0},{8,12},{12,8},{16,20},{20,16},{24,28},{28,24},{1,5},{5... | collective-permute-start | bytes 1327112 | tf_op jit(solution)/shard_map/ppermute | solution.py:17
  326.0 22.5 %collective-permute-start.47 = (bf16[256,768]{1,0:T(8,128)(2,1)}, bf16[256,768]{1,0:T(8,128)(2,1)S(1)}, u32[]{:S(2)}, u32[]{:S(2)}) collective-permute-start(bf16[256,768]{1,0:T(8,128)(2,1)} %project.20), channel_id=1, source_target_pairs={{0,16},{4,20},{8,24},{12,28},{16,0},{20,4},{24,8},{28,12},{1,17},{... | collective-permute-start | bytes 1179656 | tf_op jit(solution)/shard_map/ppermute | solution.py:17
  361.4 24.2 %collective-permute-start.52 = (bf16[240,2048]{1,0:T(8,128)(2,1)S(1)}, bf16[240,2048]{1,0:T(8,128)(2,1)S(1)}, u32[]{:S(2)}, u32[]{:S(2)}) collective-permute-start(bf16[240,2048]{1,0:T(8,128)(2,1)S(1)} %add_convert_fusion.3), channel_id=1, source_target_pairs={{0,2},{1,3},{2,0},{3,1},{4,6},{5,7},{6,4},{7,5},{8,10},{9,11},{10,... | collective-permute-start | bytes 2949128 | tf_op jit(solution)/shard_map/ppermute | solution.py:17
  364.9 28.8 %collective-permute-start.55 = (bf16[240,2048]{1,0:T(8,128)(2,1)S(1)}, bf16[240,2048]{1,0:T(8,128)(2,1)S(1)}, u32[]{:S(2)}, u32[]{:S(2)}) collective-permute-start(bf16[240,2048]{1,0:T(8,128)(2,1)S(1)} %out_block.15), channel_id=1, source_target_pairs={{0,1},{1,0},{2,3},{3,2},{4,5},{5,4},{6,7},{7,6},{8,9},{9,8},{10,11... | collective-permute-start | bytes 2949128 | tf_op jit(solution)/shard_map/ppermute | solution.py:17
  387.9 27.0 %collective-permute-start.54 = (bf16[272,2048]{1,0:T(8,128)(2,1)S(1)}, bf16[272,2048]{1,0:T(8,128)(2,1)S(1)}, u32[]{:S(2)}, u32[]{:S(2)}) collective-permute-start(bf16[272,2048]{1,0:T(8,128)(2,1)S(1)} %add_convert_fusion.1), channel_id=1, source_target_pairs={{0,2},{1,3},{2,0},{3,1},{4,6},{5,7},{6,4},{7,5},{8,10},{9,11},{10,... | collective-permute-start | bytes 3342344 | tf_op jit(solution)/shard_map/ppermute | solution.py:17
  (88 other events, 1282.7 us)
where the time goes:
time: 425 us; the launch traced here: 418 us
  waiting for transfers between devices  209 us (49%)
  Pallas kernels  75.9 us (18%)
  starting transfers between devices  62.5 us (15%)
  local copies, waits for them, and re-layouts  35.2 us (8%)
  other arithmetic  29.3 us (7%)
    ppermute x54, waiting for transfers between devices, swapped(): lax.ppermute(value, axis, [(i, i ^ bit) for i in range(lax.axis_size(axis...  209 us
    ppermute x54, starting transfers between devices, swapped(): lax.ppermute(value, axis, [(i, i ^ bit) for i in range(lax.axis_size(axis...  58.9 us
    pallas_call x12, Pallas kernels, project(): pl.pallas_call(kernel, in_specs=[smem, smem] + [vmem] * (2 + len(flat) +...  49.1 us
    pallas_call x8, Pallas kernels, out_block(): pl.pallas_call(kernel, grid_spec=pltpu.PrefetchScalarGridSpec(num_scalar_...  17.7 us
    unnamed x133, local copies, waits for them, and re-layouts  17.6 us
    pallas_call x4, Pallas kernels, gate(): pl.pallas_call(kernel, grid=(slots,), in_specs=[pl.BlockSpec((1,) + value...  9.01 us
  transfers between devices with their start and end apart: 56, of which 26 were waited for; matrix products, arithmetic and copies ran while one was open for 10% of the time, Pallas kernels for 18%

commit v1 on v0

--- a/solution.py
+++ b/solution.py
@@ -17,7 +17,7 @@
     return lax.ppermute(value, axis, [(i, i ^ bit) for i in range(lax.axis_size(axis))])
 
 
-def project(order, places, rows, sections, addend, near, ranks):
+def project(order, places, rows, sections, near, ranks):
     depth = rows[0].shape[1]
     slabs = len(sections[0])
     branches, slab, width = sections[0][0].shape
@@ -42,8 +42,6 @@
             for b in range(branches):
                 columns = slice(b * width, (b + 1) * width)
                 value = jnp.dot(part, refs[2 + i][b], preferred_element_type=jnp.float32)
-                if i == 0 and addend is not None:
-                    value += refs[2 + len(flat)][:, columns].astype(jnp.float32)
                 if i:
                     value += total[:, columns]
                 if i < len(flat) - 1:
@@ -51,12 +49,11 @@
                 else:
                     out_ref[:, columns] = value.astype(jnp.bfloat16)
 
-    extra = [] if addend is None else [addend]
     smem = pl.BlockSpec(memory_space=pltpu.SMEM)
     vmem = pl.BlockSpec(memory_space=pltpu.VMEM)
     return pl.pallas_call(
         kernel,
-        in_specs=[smem, smem] + [vmem] * (2 + len(flat) + len(extra)),
+        in_specs=[smem, smem] + [vmem] * (2 + len(flat)),
         out_specs=vmem,
         out_shape=jax.ShapeDtypeStruct((count, wide), jnp.bfloat16),
         scratch_shapes=[
@@ -66,10 +63,11 @@
         compiler_params=pltpu.CompilerParams(vmem_limit_bytes=VMEM),
         cost_estimate=SHORT,
         name="project",
-    )(order, places, *rows, *flat, *extra)
-
-
-def gate(inputs, spans, row_count, short_taps, skip_gain, toeplitz):
+    )(order, places, *rows, *flat)
+
+
+def gate(terms, spans, row_count, short_taps, skip_gain, toeplitz):
+    inputs = [value for term in terms for value in term]
     slots, _, wide = inputs[0].shape
     width = wide // 3
     filters = toeplitz.shape[1] // (2 * TAPS)
@@ -79,8 +77,13 @@
         input_refs = refs[: len(inputs)]
         taps_ref, skip_ref, toeplitz_ref, out_ref, extended = refs[len(inputs) :]
         end = 0
-        for ref, (first, last) in zip(input_refs, spans, strict=True):
-            extended[end : end + last - first] = ref[0, first:last].astype(jnp.float32)
+        used = 0
+        for term, (first, last) in zip(terms, spans, strict=True):
+            total = input_refs[used][0, first:last].astype(jnp.float32)
+            for ref in input_refs[used + 1 : used + len(term)]:
+                total += ref[0, first:last].astype(jnp.float32)
+            extended[end : end + last - first] = total.astype(jnp.bfloat16).astype(jnp.float32)
+            used += len(term)
             end += last - first
         if row_count < TAPS:
             extended[end:] = jnp.zeros((TAPS - row_count, wide), jnp.float32)
@@ -129,24 +132,31 @@
     tile = min(columns, 512)
     steps = columns // tile
 
-    def kernel(block_ref, gating_ref, w_ref, out_ref):
-        out_ref[...] = jnp.dot(
-            gating_ref[...], w_ref[...], preferred_element_type=jnp.float32
-        ).astype(jnp.bfloat16)
-
+    def kernel(block_ref, gating_ref, w_ref, out_ref, held, sems):
+        first = block_ref[0] * columns
+        loads = []
+        for i in range(steps):
+            place = pl.ds(pl.multiple_of(first + i * tile, 128), tile)
+            loads.append(pltpu.make_async_copy(w_ref.at[:, place], held.at[i], sems.at[i]))
+        for load in loads:
+            load.start()
+        for i, load in enumerate(loads):
+            load.wait()
+            out_ref[:, i * tile : (i + 1) * tile] = jnp.dot(
+                gating_ref[...], held[i], preferred_element_type=jnp.float32
+            ).astype(jnp.bfloat16)
+
+    vmem = pl.BlockSpec(memory_space=pltpu.VMEM)
     return pl.pallas_call(
         kernel,
-        grid_spec=pltpu.PrefetchScalarGridSpec(
-            num_scalar_prefetch=1,
-            grid=(steps,),
-            in_specs=[
-                pl.BlockSpec((rows, depth), lambda i, b: (0, 0)),
-                pl.BlockSpec((depth, tile), lambda i, b: (0, b[0] * steps + i)),
-            ],
-            out_specs=pl.BlockSpec((rows, tile), lambda i, b: (0, i)),
-        ),
+        in_specs=[pl.BlockSpec(memory_space=pltpu.SMEM), vmem, pl.BlockSpec(memory_space=pl.ANY)],
+        out_specs=vmem,
         out_shape=jax.ShapeDtypeStruct((rows, columns), jnp.bfloat16),
-        compiler_params=pltpu.CompilerParams(vmem_limit_bytes=VMEM),
+        scratch_shapes=[
+            pltpu.VMEM((steps, depth, tile), jnp.bfloat16),
+            pltpu.SemaphoreType.DMA((steps,)),
+        ],
+        compiler_params=pltpu.CompilerParams(vmem_limit_bytes=50 << 20),
         cost_estimate=SHORT,
         name="out_block",
     )(block.reshape(1).astype(jnp.int32), gating, w_out)
@@ -194,10 +204,10 @@
     state = {}
 
     def cut(i, o, h):
-        if h not in state:
+        if ("slab", h) not in state:
             rows = jnp.transpose(w_in[h * slab : (h + 1) * slab], (1, 0, 2))
-            state[h] = lax.optimization_barrier(rows)
-        return lax.dynamic_slice_in_dim(state[h], (place ^ o) * mine + i * width, width, 2)
+            state["slab", h] = lax.optimization_barrier(rows)
+        return lax.dynamic_slice_in_dim(state["slab", h], (place ^ o) * mine + i * width, width, 2)
 
     def near_w(i, h):
         if i < pieces:
@@ -214,23 +224,24 @@
             for o in range(1, near):
                 state["w", i, o, 1, h] = swapped(state["w", i, o, 0, h], "seq", 1)
 
-    def share():
-        cuts = []
+    def share(first_part, last_part):
         for r in range(ranks):
             rows = []
-            for first, last in parts:
+            for first, last in parts[first_part:last_part]:
                 size = (last - first) // ranks
                 rows.append(lax.dynamic_slice_in_dim(tokens, first + (column ^ r) * size, size, 0))
-            cuts.append(jnp.concatenate(rows, 0))
-        for r in range(ranks):
-            state["shared", r] = cuts[r] if r == 0 else swapped(cuts[r], "chan", r)
+            rows = jnp.concatenate(rows, 0)
+            state["shared", first_part, r] = rows if r == 0 else swapped(rows, "chan", r)
 
     def norm(j):
         if j >= len(parts):
             return
-        start = (row_count - parts[j][1]) // ranks
+        group = min(j, 1)
+        start = (parts[group][1] - parts[j][1]) // ranks
         size = (parts[j][1] - parts[j][0]) // ranks
-        widened = [state["shared", r][start : start + size].astype(jnp.float32) for r in range(ranks)]
+        widened = [
+            state["shared", group, r][start : start + size].astype(jnp.float32) for r in range(ranks)
+        ]
         square = sum(jnp.sum(piece * piece, axis=1, keepdims=True) for piece in widened)
         scale = lax.rsqrt(square / depth + EPSILON)
         gains = norm_gain.reshape(ranks, 1, depth // ranks)
@@ -271,23 +282,32 @@
         if j < len(parts):
             state["other", kind, j] = swapped(state[kind, j], "chan", 1)
 
-    def multiplied(kind, i, j, addend):
+    def multiplied(kind, i, j):
         rows = [state[kind, j], state["other", kind, j]]
         sections = [[state["w", i, o, p, h] for h in range(2)] for o in range(near) for p in range(2)]
-        return project(order, places, rows, sections, addend, near, ranks)
+        return project(order, places, rows, sections, near, ranks)
+
+    def drop(*names):
+        for key in [key for key in state if isinstance(key, tuple) and key[: len(names)] == names]:
+            del state[key]
 
     def partial(i, j):
         if i < pieces and j < len(parts):
-            state["partial", i, j] = multiplied("away", i, j, None)
+            state["partial", i, j] = multiplied("away", i, j)
+            if i == pieces - 1:
+                drop("away", j)
+                drop("other", "away", j)
 
     def send(i, j):
         if i < pieces and j < len(parts):
             state["moved", i, j] = swapped(state.pop(("partial", i, j)), "seq", 2 * near)
 
-    def add(i, j):
+    def own(i, j):
         if i < pieces and j < len(parts):
-            total = multiplied("kept", i, j, state.pop(("moved", i, j)))
-            state["sum", i, j] = total.reshape(near, parts[j][1] - parts[j][0], 3 * width)
+            state["own", i, j] = multiplied("kept", i, j)
+            if i == pieces - 1:
+                drop("kept", j)
+                drop("other", "kept", j)
 
     def constants():
         short = lax.dynamic_slice_in_dim(short_taps, place * mine, mine, 2)
@@ -306,16 +326,19 @@
         held = lax.optimization_barrier(list(state.values()))
         state.update(zip(list(state), held, strict=True))
 
-    share()
+    share(0, 1)
     pair_own_w(0, 0)
     near_w(0, 0)
     step()
-    for j in range(len(parts)):
-        norm(j)
+    norm(0)
     cross(0)
+    share(1, len(parts))
     pair_own_w(0, 1)
     near_w(0, 1)
     step()
+    for j in range(1, len(parts)):
+        norm(j)
+    drop("shared")
     cross(1)
     constants()
     near_rows("away", 0)
@@ -340,6 +363,7 @@
     near_w(1, 1)
     pair_own_w(1, 1)
     step()
+    drop("slab")
     send(0, 1)
     beside("away", 2)
     partial(0, 2)
@@ -349,6 +373,7 @@
     send(0, 2)
     across("kept", 0)
     near_rows("kept", 1)
+    near_rows("kept", 2)
     pair_near_w(1, 1)
     step()
     partial(1, 0)
@@ -356,39 +381,43 @@
     partial(1, 1)
     beside("kept", 0)
     across("kept", 1)
-    near_rows("kept", 2)
-    add(0, 0)
-    step()
-    send(1, 1)
-    beside("kept", 1)
-    across("kept", 2)
-    add(1, 0)
-    add(0, 1)
-    partial(1, 2)
-    step()
-    send(1, 2)
-    beside("kept", 2)
-
+    own(0, 0)
+    own(1, 0)
+    step()
     far = [(2 * i + 1, 2 * (near + i)) for i in range(near)]
 
+    def term(kind, i, j):
+        value = state[kind, i, j]
+        return value.reshape(near, value.shape[0] // near, 3 * width)
+
+    def edges(i):
+        edge = [term(kind, i, 0)[:, -EDGE:].astype(jnp.float32) for kind in ("own", "moved")]
+        edge = (edge[0] + edge[1]).astype(jnp.bfloat16)
+        edge = jnp.stack([lax.dynamic_index_in_dim(edge, place ^ o, 0, False) for o in range(near)])
+        state["edge", i], state["other edge", i] = edge, swapped(edge, "seq", 1)
+
     def halo(i):
-        edge = state["sum", i, 0][:, -EDGE:]
-        edge = jnp.stack([lax.dynamic_index_in_dim(edge, place ^ o, 0, False) for o in range(near)])
-        other = swapped(edge, "seq", 1)
+        edge, other = state.pop(("edge", i)), state.pop(("other edge", i))
         before = jnp.concatenate([lax.ppermute(edge[-1:], "seq", far), other[:-1]], 0)
         rows = jnp.where(odd == 1, other, before)
-        return jnp.stack([lax.dynamic_index_in_dim(rows, place ^ o, 0, False) for o in range(near)])
-
-    low = parts[-1][1] + EDGE
-
-    def gated(i, inputs, spans, rows):
-        return gate(inputs, spans, rows, *[state["constants", i, k] for k in range(3)])
-
-    def joined(gates, rows):
-        gating = jnp.zeros((rows, channels), jnp.bfloat16)
+        rows = [lax.dynamic_index_in_dim(rows, place ^ o, 0, False) for o in range(near)]
+        state["halo", i] = jnp.stack(rows)
+
+    def passed_near(value):
+        return [value[o] if o == 0 else swapped(value[o], "seq", 2 * o) for o in range(near)]
+
+    last = len(parts) - 1
+
+    def gated(i):
+        terms = [(term("own", i, j), term("moved", i, j)) for j in reversed(range(len(parts)))]
+        spans = [(0, EDGE)] + [(0, value.shape[1]) for value, _ in terms]
+        constants = [state["constants", i, k] for k in range(3)]
+        return gate([(state["halo", i],)] + terms, spans, row_count, *constants)
+
+    def joined(gates):
+        gating = jnp.zeros((row_count, channels), jnp.bfloat16)
         for o in range(near):
-            moved = [piece[o] if o == 0 else swapped(piece[o], "seq", 2 * o) for piece in gates]
-            shares = jnp.concatenate(moved, 1)
+            shares = jnp.concatenate([piece[o] for piece in gates], 1)
             gating = lax.dynamic_update_slice(gating, shares, (0, (place ^ o) * mine))
         return gating
 
@@ -400,40 +429,39 @@
     def far_sums(gating):
         return [chip_sum(gating, a).astype(jnp.bfloat16) for a in range(1, ranks // 2)]
 
-    def sent(sums):
-        return [swapped(value, "chan", 2 * a) for a, value in enumerate(sums, 1)]
-
-    def added(first, last, own, received):
-        total = tokens[first:last].astype(jnp.float32) + own
-        return (total + sum(value.astype(jnp.float32) for value in received)).astype(jnp.bfloat16)
-
-    def all_gated(i):
-        inputs = [state["sum", i, j] for j in reversed(range(len(parts) - 1))]
-        return gated(i, inputs, [(0, value.shape[1]) for value in inputs], row_count - low)
-
-    last = len(parts) - 1
-    add(1, 1)
-    upper = joined([all_gated(i) for i in range(pieces)], row_count - low)
-    upper, *first_halos = lax.optimization_barrier([upper] + [halo(i) for i in range(pieces)])
-    upper_sums = far_sums(upper)
+    send(1, 1)
+    beside("kept", 1)
+    across("kept", 2)
+    partial(1, 2)
+    own(0, 1)
+    own(1, 1)
     for i in range(pieces):
-        if i:
-            state["moved", i, last], upper_sums = lax.optimization_barrier((state["moved", i, last], upper_sums))
-    upper_received = sent(upper_sums)
-    lower = []
+        edges(i)
+    step()
+    send(1, 2)
+    beside("kept", 2)
     for i in range(pieces):
-        if last > 1 or i:
-            add(i, last)
-        lowest, next_up = state["sum", i, last], state["sum", i, last - 1]
-        spans = [(0, EDGE), (0, lowest.shape[1]), (0, EDGE)]
-        lower.append(gated(i, [first_halos[i], lowest, next_up], spans, low))
-    lower = joined(lower, low)
-    lower_sums = far_sums(lower)
-    lower_sums, upper_received, lower = lax.optimization_barrier((lower_sums, upper_received, lower))
-    lower_received = sent(lower_sums)
-    upper = added(low, row_count, chip_sum(upper, 0), upper_received)
-    lower = added(0, low, chip_sum(lower, 0), lower_received)
-    return jnp.concatenate([lower, upper], 0)
+        halo(i)
+    if last > 1:
+        own(0, last)
+        own(1, last)
+    drop("w")
+    if pieces > 1:
+        state["gated"] = passed_near(gated(0))
+    step()
+    gates = [state["gated"]] if pieces > 1 else []
+    for i in range(len(gates), pieces):
+        gates.append(passed_near(gated(i)))
+    gating = joined(gates)
+    state["gating"] = gating
+    state["sums"] = far_sums(gating)
+    state["block"] = out_block(gating, w_out, column ^ 1, ranks)
+    step()
+    received = [swapped(value, "chan", 2 * a) for a, value in enumerate(state["sums"], 1)]
+    received.append(swapped(state["block"], "chan", 1))
+    total = tokens.astype(jnp.float32)
+    total += out_block(state["gating"], w_out, column, ranks).astype(jnp.float32)
+    return (total + sum(value.astype(jnp.float32) for value in received)).astype(jnp.bfloat16)
 
 
 def solution(mesh):

time: 425 us -> 415 us (0.976)
  Pallas kernels: 75.9 us -> 69.8 us
  other arithmetic: 29.3 us -> 23.2 us
  starting transfers between devices: 62.5 us -> 67.9 us
  waiting for transfers between devices: 209 us -> 214 us
  local copies, waits for them, and re-layouts: 35.2 us -> 30.8 us
    unnamed x133 -> x177, local copies, waits for them, and re-layouts: 17.6 us -> 11.2 us
    ppermute x54 -> x52, starting transfers between devices: 58.9 us -> 65 us  [swapped(): lax.ppermute(value, axis, [(i, i ^ bit) for i in range(lax.axis_size(axis...]
    pallas_call x20 -> x16, Pallas kernels: 66.9 us -> 61.9 us  [the longest x12 45.5 us: project(): pl.pallas_call(kernel, in_specs=[smem, smem] + [vmem] * (2 + len(flat)),...]
    concatenate x5 -> x4, other arithmetic: 5.06 us -> 0.1 us  [share(): rows = jnp.concatenate(rows, 0)]
    convert_element_type x2 -> x3, other arithmetic: 1.53 us -> 5.87 us  [the longest x1 3.28 us: per_device(): (total + sum((value.astype(jnp.float32) for value in received))).astype(j...]
    ppermute x54 -> x52, waiting for transfers between devices: 209 us -> 211 us  [swapped(): lax.ppermute(value, axis, [(i, i ^ bit) for i in range(lax.axis_size(axis...]
    pallas_call x4 -> x2, Pallas kernels: 9.01 us -> 7.91 us  [gate(): pl.pallas_call(kernel, grid=(slots,), in_specs=[pl.BlockSpec((1,) + value...]
  transfers between devices with their start and end apart: 56 -> 54, of which waited for: 26 -> 25; matrix products, arithmetic and copies ran while one was open for 10% -> 10% of each run, Pallas kernels for 18% -> 15%
where the time goes in v1:
time: 415 us; the launch traced here: 411 us
  waiting for transfers between devices  214 us (52%)
  Pallas kernels  69.8 us (17%)
  starting transfers between devices  67.9 us (16%)
  local copies, waits for them, and re-layouts  30.8 us (7%)
  other arithmetic  23.2 us (6%)
    ppermute x52, waiting for transfers between devices, swapped(): lax.ppermute(value, axis, [(i, i ^ bit) for i in range(lax.axis_size(axis...  211 us
    ppermute x52, starting transfers between devices, swapped(): lax.ppermute(value, axis, [(i, i ^ bit) for i in range(lax.axis_size(axis...  65 us
    pallas_call x12, Pallas kernels, project(): pl.pallas_call(kernel, in_specs=[smem, smem] + [vmem] * (2 + len(flat)),...  45.5 us
    pallas_call x4, Pallas kernels, out_block(): pl.pallas_call(kernel, in_specs=[pl.BlockSpec(memory_space=pltpu.SMEM), v...  16.4 us
    unnamed x177, local copies, waits for them, and re-layouts  11.2 us
  transfers between devices with their start and end apart: 54, of which 25 were waited for; matrix products, arithmetic and copies ran while one was open for 10% of the time, Pallas kernels for 15%

profile of v1, /device:TPU:4, one launch (start us, length us, event | category | flops | bytes accessed | tf_op | source)
XLA Modules:
  0.0 411.2 jit_solution(7822714435752162767)
XLA Ops:
  4.3 6.8 %slice_bitcast_fusion = (bf16[3,512,1024]{2,1,0:T(8,128)(2,1)}, bf16[3,512,1024]{2,1,0:T(8,128)(2,1)}) fusion(bf16[1024,3,1024]{2,0,1:T(8,128)(2,1)} %param.9), kind=kLoop, calls=%fused_computation.5 | loop fusion | bytes 12582912 | tf_op jit(solution)/shard_map/transpose | solution.py:208
  15.8 3.8 fusion.2
  27.5 5.9 %collective-permute-done.4.refs_6_ = bf16[3,512,256]{2,1,0:T(8,128)(2,1)S(1)} collective-permute-done((bf16[3,512,256]{2,1,0:T(8,128)(2,1)}, bf16[3,512,256]{2,1,0:T(8,128)(2,1)S(1)}, u32[]{:S(2)}, u32[]{:S(2)}) %collective-permute-start.4) | collective-permute-done | bytes 786464 | tf_op jit(solution)/shard_map/ppermute | solution.py:17
  42.9 17.7 %collective-permute-done.10.refs_7_ = bf16[3,512,256]{2,1,0:T(8,128)(2,1)S(1)} collective-permute-done((bf16[3,512,256]{2,1,0:T(8,128)(2,1)S(1)}, bf16[3,512,256]{2,1,0:T(8,128)(2,1)S(1)}, u32[]{:S(2)}, u32[]{:S(2)}) %collective-permute-start.10) | collective-permute-done | bytes 786464 | tf_op jit(solution)/shard_map/ppermute | solution.py:17
  68.3 10.1 %collective-permute-done.11 = bf16[48,4096]{1,0:T(8,128)(2,1)S(1)} collective-permute-done((bf16[48,4096]{1,0:T(8,128)(2,1)S(1)}, bf16[48,4096]{1,0:T(8,128)(2,1)S(1)}, u32[]{:S(2)}, u32[]{:S(2)}) %collective-permute-start.11) | collective-permute-done | bytes 393248 | tf_op jit(solution)/shard_map/ppermute | solution.py:17
  78.5 5.5 %collective-permute-done.12 = bf16[48,4096]{1,0:T(8,128)(2,1)S(1)} collective-permute-done((bf16[48,4096]{1,0:T(8,128)(2,1)S(1)}, bf16[48,4096]{1,0:T(8,128)(2,1)S(1)}, u32[]{:S(2)}, u32[]{:S(2)}) %collective-permute-start.12) | collective-permute-done | bytes 393248 | tf_op jit(solution)/shard_map/ppermute | solution.py:17
  87.7 10.3 %collective-permute-done.15 = bf16[48,4096]{1,0:T(8,128)(2,1)S(1)} collective-permute-done((bf16[48,4096]{1,0:T(8,128)(2,1)S(1)}, bf16[48,4096]{1,0:T(8,128)(2,1)S(1)}, u32[]{:S(2)}, u32[]{:S(2)}) %collective-permute-start.15) | collective-permute-done | bytes 393248 | tf_op jit(solution)/shard_map/ppermute | solution.py:17
  109.0 5.1 %collective-permute-done.19 = bf16[32,4096]{1,0:T(8,128)(2,1)S(1)} collective-permute-done((bf16[32,4096]{1,0:T(8,128)(2,1)}, bf16[32,4096]{1,0:T(8,128)(2,1)S(1)}, u32[]{:S(2)}, u32[]{:S(2)}) %collective-permute-start.19) | collective-permute-done | bytes 262176 | tf_op jit(solution)/shard_map/ppermute | solution.py:17
  114.1 10.0 %collective-permute-done.18 = bf16[96,4096]{1,0:T(8,128)(2,1)} collective-permute-done((bf16[96,4096]{1,0:T(8,128)(2,1)}, bf16[96,4096]{1,0:T(8,128)(2,1)}, u32[]{:S(2)}, u32[]{:S(2)}) %collective-permute-start.18) | collective-permute-done | bytes 786464 | tf_op jit(solution)/shard_map/ppermute | solution.py:17
  125.7 4.9 %project.12 = bf16[384,768]{1,0:T(8,128)(2,1)S(1)} custom-call(s32[4]{0:T(128)S(1)} %get-tuple-element.619.order_ref, s32[4]{0:T(128)S(1)} %get-tuple-element.620.places_ref, bf16[192,4096]{1,0:T(8,128)(2,1)} %pad_maximum_fusion.refs_0_, bf16[192,4096]{1,0:T(8,128)(2,1)} %collective-permute-done.20.refs_1_, ...), custom_call_target="tpu_custom_call" | custom-call | flops 1 | bytes 1 | tf_op jit(solution)/shard_map/project/pallas_call | solution.py:54
  135.5 9.5 %collective-permute-done.23 = bf16[64,4096]{1,0:T(8,128)(2,1)S(1)} collective-permute-done((bf16[64,4096]{1,0:T(8,128)(2,1)S(1)}, bf16[64,4096]{1,0:T(8,128)(2,1)S(1)}, u32[]{:S(2)}, u32[]{:S(2)}) %collective-permute-start.23) | collective-permute-done | bytes 524320 | tf_op jit(solution)/shard_map/ppermute | solution.py:17
  148.5 14.9 %collective-permute-done.24 = bf16[384,768]{1,0:T(8,128)(2,1)S(1)} collective-permute-done((bf16[384,768]{1,0:T(8,128)(2,1)S(1)}, bf16[384,768]{1,0:T(8,128)(2,1)S(1)}, u32[]{:S(2)}, u32[]{:S(2)}) %collective-permute-start.24) | collective-permute-done | bytes 589856 | tf_op jit(solution)/shard_map/ppermute | solution.py:17
  168.3 16.2 %collective-permute-done.28 = bf16[48,4096]{1,0:T(8,128)(2,1)S(1)} collective-permute-done((bf16[48,4096]{1,0:T(8,128)(2,1)S(1)}, bf16[48,4096]{1,0:T(8,128)(2,1)S(1)}, u32[]{:S(2)}, u32[]{:S(2)}) %collective-permute-start.28) | collective-permute-done | bytes 393248 | tf_op jit(solution)/shard_map/ppermute | solution.py:17
  187.5 8.4 %collective-permute-done.29 = bf16[384,768]{1,0:T(8,128)(2,1)S(1)} collective-permute-done((bf16[384,768]{1,0:T(8,128)(2,1)S(1)}, bf16[384,768]{1,0:T(8,128)(2,1)S(1)}, u32[]{:S(2)}, u32[]{:S(2)}) %collective-permute-start.29) | collective-permute-done | bytes 589856 | tf_op jit(solution)/shard_map/ppermute | solution.py:17
  201.5 8.3 %collective-permute-done.34 = bf16[32,4096]{1,0:T(8,128)(2,1)S(1)} collective-permute-done((bf16[32,4096]{1,0:T(8,128)(2,1)S(1)}, bf16[32,4096]{1,0:T(8,128)(2,1)S(1)}, u32[]{:S(2)}, u32[]{:S(2)}) %collective-permute-start.34) | collective-permute-done | bytes 262176 | tf_op jit(solution)/shard_map/ppermute | solution.py:17
  210.7 9.4 %collective-permute-done.33 = bf16[48,4096]{1,0:T(8,128)(2,1)S(1)} collective-permute-done((bf16[48,4096]{1,0:T(8,128)(2,1)S(1)}, bf16[48,4096]{1,0:T(8,128)(2,1)S(1)}, u32[]{:S(2)}, u32[]{:S(2)}) %collective-permute-start.33) | collective-permute-done | bytes 393248 | tf_op jit(solution)/shard_map/ppermute | solution.py:17
  222.0 4.7 %project.15 = bf16[384,768]{1,0:T(8,128)(2,1)S(1)} custom-call(s32[4]{0:T(128)S(1)} %get-tuple-element.619.order_ref, s32[4]{0:T(128)S(1)} %get-tuple-element.620.places_ref, bf16[192,4096]{1,0:T(8,128)(2,1)} %pad_maximum_fusion.refs_0_, bf16[192,4096]{1,0:T(8,128)(2,1)} %collective-permute-done.20.refs_1_, ...), custom_call_target="tpu_custom_call" | custom-call | flops 1 | bytes 1 | tf_op jit(solution)/shard_map/project/pallas_call | solution.py:54
  231.5 9.5 %collective-permute-done.37 = bf16[96,4096]{1,0:T(8,128)(2,1)S(1)} collective-permute-done((bf16[96,4096]{1,0:T(8,128)(2,1)S(1)}, bf16[96,4096]{1,0:T(8,128)(2,1)S(1)}, u32[]{:S(2)}, u32[]{:S(2)}) %collective-permute-start.37) | collective-permute-done | bytes 786464 | tf_op jit(solution)/shard_map/ppermute | solution.py:17
  250.0 5.6 %collective-permute-done.38 = bf16[384,768]{1,0:T(8,128)(2,1)S(1)} collective-permute-done((bf16[384,768]{1,0:T(8,128)(2,1)S(1)}, bf16[384,768]{1,0:T(8,128)(2,1)S(1)}, u32[]{:S(2)}, u32[]{:S(2)}) %collective-permute-start.38) | collective-permute-done | bytes 589856 | tf_op jit(solution)/shard_map/ppermute | solution.py:17
  272.1 4.9 %project.21 = bf16[384,768]{1,0:T(8,128)(2,1)S(1)} custom-call(s32[4]{0:T(128)S(1)} %get-tuple-element.619.order_ref, s32[4]{0:T(128)S(1)} %get-tuple-element.620.places_ref, bf16[192,4096]{1,0:T(8,128)(2,1)} %pad_maximum_fusion.3.refs_0_, bf16[192,4096]{1,0:T(8,128)(2,1)} %collective-permute-done.42.refs_1_, ...), custom_call_target="tpu_custom_call" | custom-call | flops 1 | bytes 1 | tf_op jit(solution)/shard_map/project/pallas_call | solution.py:54
  277.0 4.9 %project.20 = bf16[384,768]{1,0:T(8,128)(2,1)S(1)} custom-call(s32[4]{0:T(128)S(1)} %get-tuple-element.619.order_ref, s32[4]{0:T(128)S(1)} %get-tuple-element.620.places_ref, bf16[192,4096]{1,0:T(8,128)(2,1)} %pad_maximum_fusion.3.refs_0_, bf16[192,4096]{1,0:T(8,128)(2,1)} %collective-permute-done.42.refs_1_, ...), custom_call_target="tpu_custom_call" | custom-call | flops 1 | bytes 1 | tf_op jit(solution)/shard_map/project/pallas_call | solution.py:54
  282.8 6.6 %collective-permute-done.41 = bf16[384,768]{1,0:T(8,128)(2,1)S(1)} collective-permute-done((bf16[384,768]{1,0:T(8,128)(2,1)}, bf16[384,768]{1,0:T(8,128)(2,1)S(1)}, u32[]{:S(2)}, u32[]{:S(2)}) %collective-permute-start.41) | collective-permute-done | bytes 589856 | tf_op jit(solution)/shard_map/ppermute | solution.py:17
  300.9 3.7 project.22
  304.6 3.9 gate.2
  308.6 19.2 %collective-permute-start.49 = (bf16[512,256]{1,0:T(8,128)(2,1)S(1)}, bf16[512,256]{1,0:T(8,128)(2,1)S(1)}, u32[]{:S(2)}, u32[]{:S(2)}) collective-permute-start(bf16[512,256]{1,0:T(8,128)(2,1)S(1)} %get-tuple-element.585), channel_id=1, source_target_pairs={{0,8},{4,12},{8,0},{12,4},{16,24},{20,28},{24,16},{28,20},{1,9},{5... | collective-permute-start | bytes 786440 | tf_op jit(solution)/shard_map/ppermute | solution.py:17
  334.3 4.1 gate.3
  340.4 5.8 %collective-permute-done.50 = bf16[512,256]{1,0:T(8,128)(2,1)S(1)} collective-permute-done((bf16[512,256]{1,0:T(8,128)(2,1)S(1)}, bf16[512,256]{1,0:T(8,128)(2,1)S(1)}, u32[]{:S(2)}, u32[]{:S(2)}) %collective-permute-start.50) | collective-permute-done | bytes 262176 | tf_op jit(solution)/shard_map/ppermute | solution.py:17
  346.3 4.1 out_block.5
  350.4 4.1 out_block.6
  354.6 4.1 out_block.4
  360.7 4.1 out_block.7
  364.8 42.8 %collective-permute-done.52 = bf16[512,2048]{1,0:T(8,128)(2,1)S(1)} collective-permute-done((bf16[512,2048]{1,0:T(8,128)(2,1)S(1)}, bf16[512,2048]{1,0:T(8,128)(2,1)S(1)}, u32[]{:S(2)}, u32[]{:S(2)}) %collective-permute-start.52) | collective-permute-done | bytes 2097184 | tf_op jit(solution)/shard_map/ppermute | solution.py:17
  (353 shorter events, 130.6 us)
Async XLA Ops:
  2.5 23.0 %collective-permute-start.2 = (bf16[48,2048]{1,0:T(8,128)(2,1)}, bf16[48,2048]{1,0:T(8,128)(2,1)}, u32[]{:S(2)}, u32[]{:S(2)}) collective-permute-start(bf16[48,2048]{1,0:T(8,128)(2,1)} %get-tuple-element.567), channel_id=1, source_target_pairs={{0,3},{1,2},{2,1},{3,0},{4,7},{5,6},{6,5},{7,4},{8,11},{9,10},{10,... | collective-permute-start | bytes 589832 | tf_op jit(solution)/shard_map/ppermute | solution.py:17
  3.4 22.2 %collective-permute-start.1 = (bf16[48,2048]{1,0:T(8,128)(2,1)}, bf16[48,2048]{1,0:T(8,128)(2,1)}, u32[]{:S(2)}, u32[]{:S(2)}) collective-permute-start(bf16[48,2048]{1,0:T(8,128)(2,1)} %get-tuple-element.568), channel_id=1, source_target_pairs={{0,2},{1,3},{2,0},{3,1},{4,6},{5,7},{6,4},{7,5},{8,10},{9,11},{10,... | collective-permute-start | bytes 589832 | tf_op jit(solution)/shard_map/ppermute | solution.py:17
  4.0 23.1 %collective-permute-start = (bf16[48,2048]{1,0:T(8,128)(2,1)}, bf16[48,2048]{1,0:T(8,128)(2,1)}, u32[]{:S(2)}, u32[]{:S(2)}) collective-permute-start(bf16[48,2048]{1,0:T(8,128)(2,1)} %get-tuple-element.569), channel_id=1, source_target_pairs={{0,1},{1,0},{2,3},{3,2},{4,5},{5,4},{6,7},{7,6},{8,9},{9,8},{10,11... | collective-permute-start | bytes 589832 | tf_op jit(solution)/shard_map/ppermute | solution.py:17
  33.4 27.2 %collective-permute-start.10 = (bf16[3,512,256]{2,1,0:T(8,128)(2,1)S(1)}, bf16[3,512,256]{2,1,0:T(8,128)(2,1)S(1)}, u32[]{:S(2)}, u32[]{:S(2)}) collective-permute-start(bf16[3,512,256]{2,1,0:T(8,128)(2,1)S(1)} %get-tuple-element.557), channel_id=1, source_target_pairs={{0,8},{4,12},{8,0},{12,4},{16,24},{20,28},{24,16},{28,20},{1,9},{5... | collective-permute-start | bytes 2359304 | tf_op jit(solution)/shard_map/ppermute | solution.py:17
  35.0 25.7 %collective-permute-start.9 = (bf16[3,512,256]{2,1,0:T(8,128)(2,1)S(1)}, bf16[3,512,256]{2,1,0:T(8,128)(2,1)S(1)}, u32[]{:S(2)}, u32[]{:S(2)}) collective-permute-start(bf16[3,512,256]{2,1,0:T(8,128)(2,1)S(1)} %get-tuple-element.521.refs_3_), channel_id=1, source_target_pairs={{0,4},{4,0},{8,12},{12,8},{16,20},{20,16},{24,28},{28,24},{1,5},{5... | collective-permute-start | bytes 2359304 | tf_op jit(solution)/shard_map/ppermute | solution.py:17
  39.5 21.2 %collective-permute-start.5 = (bf16[48,4096]{1,0:T(8,128)(2,1)S(1)}, bf16[48,4096]{1,0:T(8,128)(2,1)S(1)}, u32[]{:S(2)}, u32[]{:S(2)}) collective-permute-start(bf16[48,4096]{1,0:T(8,128)(2,1)S(1)} %pad_maximum_fusion.20), channel_id=1, source_target_pairs={{0,16},{4,20},{8,24},{12,28},{16,0},{20,4},{24,8},{28,12},{1,17},{... | collective-permute-start | bytes 1179656 | tf_op jit(solution)/shard_map/ppermute | solution.py:17
  103.8 21.8 %collective-permute-start.20 = (bf16[192,4096]{1,0:T(8,128)(2,1)}, bf16[192,4096]{1,0:T(8,128)(2,1)}, u32[]{:S(2)}, u32[]{:S(2)}) collective-permute-start(bf16[192,4096]{1,0:T(8,128)(2,1)} %pad_maximum_fusion.refs_0_), channel_id=1, source_target_pairs={{0,1},{1,0},{2,3},{3,2},{4,5},{5,4},{6,7},{7,6},{8,9},{9,8},{10,11... | collective-permute-start | bytes 4718600 | tf_op jit(solution)/shard_map/ppermute | solution.py:17
  103.8 20.3 %collective-permute-start.18 = (bf16[96,4096]{1,0:T(8,128)(2,1)}, bf16[96,4096]{1,0:T(8,128)(2,1)}, u32[]{:S(2)}, u32[]{:S(2)}) collective-permute-start(bf16[96,4096]{1,0:T(8,128)(2,1)} %pad_maximum_fusion.9), channel_id=1, source_target_pairs={{0,2},{1,3},{2,0},{3,1},{4,6},{5,7},{6,4},{7,5},{8,10},{9,11},{10,... | collective-permute-start | bytes 2359304 | tf_op jit(solution)/shard_map/ppermute | solution.py:17
  108.0 22.6 %collective-permute-start.21 = (bf16[3,512,256]{2,1,0:T(8,128)(2,1)S(1)}, bf16[3,512,256]{2,1,0:T(8,128)(2,1)S(1)}, u32[]{:S(2)}, u32[]{:S(2)}) collective-permute-start(bf16[3,512,256]{2,1,0:T(8,128)(2,1)S(1)} %get-tuple-element.556), channel_id=1, source_target_pairs={{0,8},{4,12},{8,0},{12,4},{16,24},{20,28},{24,16},{28,20},{1,9},{5... | collective-permute-start | bytes 2359304 | tf_op jit(solution)/shard_map/ppermute | solution.py:17
  108.4 22.2 %collective-permute-start.22 = (bf16[3,512,256]{2,1,0:T(8,128)(2,1)S(1)}, bf16[3,512,256]{2,1,0:T(8,128)(2,1)S(1)}, u32[]{:S(2)}, u32[]{:S(2)}) collective-permute-start(bf16[3,512,256]{2,1,0:T(8,128)(2,1)S(1)} %get-tuple-element.528.refs_2_), channel_id=1, source_target_pairs={{0,4},{4,0},{8,12},{12,8},{16,20},{20,16},{24,28},{28,24},{1,5},{5... | collective-permute-start | bytes 2359304 | tf_op jit(solution)/shard_map/ppermute | solution.py:17
  131.9 32.3 %collective-permute-start.26 = (bf16[3,512,256]{2,1,0:T(8,128)(2,1)S(1)}, bf16[3,512,256]{2,1,0:T(8,128)(2,1)S(1)}, u32[]{:S(2)}, u32[]{:S(2)}) collective-permute-start(bf16[3,512,256]{2,1,0:T(8,128)(2,1)S(1)} %get-tuple-element.554), channel_id=1, source_target_pairs={{0,8},{4,12},{8,0},{12,4},{16,24},{20,28},{24,16},{28,20},{1,9},{5... | collective-permute-start | bytes 2359304 | tf_op jit(solution)/shard_map/ppermute | solution.py:17
  133.7 30.6 %collective-permute-start.27 = (bf16[3,512,256]{2,1,0:T(8,128)(2,1)S(1)}, bf16[3,512,256]{2,1,0:T(8,128)(2,1)S(1)}, u32[]{:S(2)}, u32[]{:S(2)}) collective-permute-start(bf16[3,512,256]{2,1,0:T(8,128)(2,1)S(1)} %get-tuple-element.529.refs_3_), channel_id=1, source_target_pairs={{0,4},{4,0},{8,12},{12,8},{16,20},{20,16},{24,28},{28,24},{1,5},{5... | collective-permute-start | bytes 2359304 | tf_op jit(solution)/shard_map/ppermute | solution.py:17
  134.2 29.3 %collective-permute-start.24 = (bf16[384,768]{1,0:T(8,128)(2,1)S(1)}, bf16[384,768]{1,0:T(8,128)(2,1)S(1)}, u32[]{:S(2)}, u32[]{:S(2)}) collective-permute-start(bf16[384,768]{1,0:T(8,128)(2,1)S(1)} %project.12), channel_id=1, source_target_pairs={{0,16},{4,20},{8,24},{12,28},{16,0},{20,4},{24,8},{28,12},{1,17},{... | collective-permute-start | bytes 1769480 | tf_op jit(solution)/shard_map/ppermute | solution.py:17
  164.3 20.3 %collective-permute-start.30 = (bf16[128,4096]{1,0:T(8,128)(2,1)S(1)}, bf16[128,4096]{1,0:T(8,128)(2,1)S(1)}, u32[]{:S(2)}, u32[]{:S(2)}) collective-permute-start(bf16[128,4096]{1,0:T(8,128)(2,1)S(1)} %pad_maximum_fusion.4.refs_0_), channel_id=1, source_target_pairs={{0,1},{1,0},{2,3},{3,2},{4,5},{5,4},{6,7},{7,6},{8,9},{9,8},{10,11... | collective-permute-start | bytes 3145736 | tf_op jit(solution)/shard_map/ppermute | solution.py:17
  164.3 20.2 %collective-permute-start.28 = (bf16[48,4096]{1,0:T(8,128)(2,1)S(1)}, bf16[48,4096]{1,0:T(8,128)(2,1)S(1)}, u32[]{:S(2)}, u32[]{:S(2)}) collective-permute-start(bf16[48,4096]{1,0:T(8,128)(2,1)S(1)} %copy-done.73), channel_id=1, source_target_pairs={{0,8},{4,12},{8,0},{12,4},{16,24},{20,28},{24,16},{28,20},{1,9},{5... | collective-permute-start | bytes 1179656 | tf_op jit(solution)/shard_map/ppermute | solution.py:17
  166.7 29.2 %collective-permute-start.31 = (bf16[3,512,256]{2,1,0:T(8,128)(2,1)S(1)}, bf16[3,512,256]{2,1,0:T(8,128)(2,1)S(1)}, u32[]{:S(2)}, u32[]{:S(2)}) collective-permute-start(bf16[3,512,256]{2,1,0:T(8,128)(2,1)S(1)} %collective-permute-done.21.refs_6_), channel_id=1, source_target_pairs={{0,4},{4,0},{8,12},{12,8},{16,20},{20,16},{24,28},{28,24},{1,5},{5... | collective-permute-start | bytes 2359304 | tf_op jit(solution)/shard_map/ppermute | solution.py:17
  167.2 28.7 %collective-permute-start.29 = (bf16[384,768]{1,0:T(8,128)(2,1)S(1)}, bf16[384,768]{1,0:T(8,128)(2,1)S(1)}, u32[]{:S(2)}, u32[]{:S(2)}) collective-permute-start(bf16[384,768]{1,0:T(8,128)(2,1)S(1)} %project.13), channel_id=1, source_target_pairs={{0,16},{4,20},{8,24},{12,28},{16,0},{20,4},{24,8},{28,12},{1,17},{... | collective-permute-start | bytes 1769480 | tf_op jit(solution)/shard_map/ppermute | solution.py:17
  196.0 24.3 %collective-permute-start.35 = (bf16[256,768]{1,0:T(8,128)(2,1)S(1)}, bf16[256,768]{1,0:T(8,128)(2,1)S(1)}, u32[]{:S(2)}, u32[]{:S(2)}) collective-permute-start(bf16[256,768]{1,0:T(8,128)(2,1)S(1)} %project.14), channel_id=1, source_target_pairs={{0,16},{4,20},{8,24},{12,28},{16,0},{20,4},{24,8},{28,12},{1,17},{... | collective-permute-start | bytes 1179656 | tf_op jit(solution)/shard_map/ppermute | solution.py:17
  199.0 21.1 %collective-permute-start.33 = (bf16[48,4096]{1,0:T(8,128)(2,1)S(1)}, bf16[48,4096]{1,0:T(8,128)(2,1)S(1)}, u32[]{:S(2)}, u32[]{:S(2)}) collective-permute-start(bf16[48,4096]{1,0:T(8,128)(2,1)S(1)} %copy-done.74), channel_id=1, source_target_pairs={{0,8},{4,12},{8,0},{12,4},{16,24},{20,28},{24,16},{28,20},{1,9},{5... | collective-permute-start | bytes 1179656 | tf_op jit(solution)/shard_map/ppermute | solution.py:17
  199.1 21.1 %collective-permute-start.32 = (bf16[96,4096]{1,0:T(8,128)(2,1)S(1)}, bf16[96,4096]{1,0:T(8,128)(2,1)S(1)}, u32[]{:S(2)}, u32[]{:S(2)}) collective-permute-start(bf16[96,4096]{1,0:T(8,128)(2,1)S(1)} %pad_maximum_fusion.10), channel_id=1, source_target_pairs={{0,2},{1,3},{2,0},{3,1},{4,6},{5,7},{6,4},{7,5},{8,10},{9,11},{10,... | collective-permute-start | bytes 2359304 | tf_op jit(solution)/shard_map/ppermute | solution.py:17
  200.0 21.1 %collective-permute-start.36 = (bf16[3,512,256]{2,1,0:T(8,128)(2,1)S(1)}, bf16[3,512,256]{2,1,0:T(8,128)(2,1)S(1)}, u32[]{:S(2)}, u32[]{:S(2)}) collective-permute-start(bf16[3,512,256]{2,1,0:T(8,128)(2,1)S(1)} %collective-permute-done.26.refs_7_), channel_id=1, source_target_pairs={{0,4},{4,0},{8,12},{12,8},{16,20},{20,16},{24,28},{28,24},{1,5},{5... | collective-permute-start | bytes 2359304 | tf_op jit(solution)/shard_map/ppermute | solution.py:17
  221.1 21.3 %collective-permute-start.39 = (bf16[192,4096]{1,0:T(8,128)(2,1)S(1)}, bf16[192,4096]{1,0:T(8,128)(2,1)S(1)}, u32[]{:S(2)}, u32[]{:S(2)}) collective-permute-start(bf16[192,4096]{1,0:T(8,128)(2,1)S(1)} %pad_maximum_fusion.2.refs_0_), channel_id=1, source_target_pairs={{0,1},{1,0},{2,3},{3,2},{4,5},{5,4},{6,7},{7,6},{8,9},{9,8},{10,11... | collective-permute-start | bytes 4718600 | tf_op jit(solution)/shard_map/ppermute | solution.py:17
  221.1 20.0 %collective-permute-start.37 = (bf16[96,4096]{1,0:T(8,128)(2,1)S(1)}, bf16[96,4096]{1,0:T(8,128)(2,1)S(1)}, u32[]{:S(2)}, u32[]{:S(2)}) collective-permute-start(bf16[96,4096]{1,0:T(8,128)(2,1)S(1)} %pad_maximum_fusion.11), channel_id=1, source_target_pairs={{0,2},{1,3},{2,0},{3,1},{4,6},{5,7},{6,4},{7,5},{8,10},{9,11},{10,... | collective-permute-start | bytes 2359304 | tf_op jit(solution)/shard_map/ppermute | solution.py:17
  226.7 28.8 %collective-permute-start.38 = (bf16[384,768]{1,0:T(8,128)(2,1)S(1)}, bf16[384,768]{1,0:T(8,128)(2,1)S(1)}, u32[]{:S(2)}, u32[]{:S(2)}) collective-permute-start(bf16[384,768]{1,0:T(8,128)(2,1)S(1)} %project.15), channel_id=1, source_target_pairs={{0,16},{4,20},{8,24},{12,28},{16,0},{20,4},{24,8},{28,12},{1,17},{... | collective-permute-start | bytes 1769480 | tf_op jit(solution)/shard_map/ppermute | solution.py:17
  259.2 23.6 %collective-permute-start.43 = (bf16[2,144,768]{2,1,0:T(8,128)(2,1)S(1)}, bf16[2,144,768]{2,1,0:T(8,128)(2,1)S(1)}, u32[]{:S(2)}, u32[]{:S(2)}) collective-permute-start(bf16[2,144,768]{2,1,0:T(8,128)(2,1)S(1)} %pad_maximum_fusion.15), channel_id=1, source_target_pairs={{0,4},{4,0},{8,12},{12,8},{16,20},{20,16},{24,28},{28,24},{1,5},{5... | collective-permute-start | bytes 1327112 | tf_op jit(solution)/shard_map/ppermute | solution.py:17
  260.7 28.7 %collective-permute-start.41 = (bf16[384,768]{1,0:T(8,128)(2,1)}, bf16[384,768]{1,0:T(8,128)(2,1)S(1)}, u32[]{:S(2)}, u32[]{:S(2)}) collective-permute-start(bf16[384,768]{1,0:T(8,128)(2,1)} %copy-done.66), channel_id=1, source_target_pairs={{0,16},{4,20},{8,24},{12,28},{16,0},{20,4},{24,8},{28,12},{1,17},{... | collective-permute-start | bytes 1769480 | tf_op jit(solution)/shard_map/ppermute | solution.py:17
  262.3 20.5 %collective-permute-start.44 = (bf16[2,144,768]{2,1,0:T(8,128)(2,1)S(1)}, bf16[2,144,768]{2,1,0:T(8,128)(2,1)S(1)}, u32[]{:S(2)}, u32[]{:S(2)}) collective-permute-start(bf16[2,144,768]{2,1,0:T(8,128)(2,1)S(1)} %pad_maximum_fusion.16), channel_id=1, source_target_pairs={{0,4},{4,0},{8,12},{12,8},{16,20},{20,16},{24,28},{28,24},{1,5},{5... | collective-permute-start | bytes 1327112 | tf_op jit(solution)/shard_map/ppermute | solution.py:17
  294.5 33.2 %collective-permute-start.47 = (bf16[1,144,768]{2,1,0:T(8,128)(2,1)S(1)}, bf16[1,144,768]{2,1,0:T(8,128)(2,1)S(1)}, u32[]{:S(2)}, u32[]{:S(2)}) collective-permute-start(bf16[1,144,768]{2,1,0:T(8,128)(2,1)S(1)} %slice.106), channel_id=1, source_target_pairs={{4,16},{12,24},{5,17},{13,25},{6,18},{14,26},{7,19},{15,27}} | collective-permute-start | bytes 663560 | tf_op jit(solution)/shard_map/ppermute | solution.py:401
  296.0 35.7 %collective-permute-start.45 = (bf16[256,768]{1,0:T(8,128)(2,1)}, bf16[256,768]{1,0:T(8,128)(2,1)S(1)}, u32[]{:S(2)}, u32[]{:S(2)}) collective-permute-start(bf16[256,768]{1,0:T(8,128)(2,1)} %copy-done.67), channel_id=1, source_target_pairs={{0,16},{4,20},{8,24},{12,28},{16,0},{20,4},{24,8},{28,12},{1,17},{... | collective-permute-start | bytes 1179656 | tf_op jit(solution)/shard_map/ppermute | solution.py:17
  308.6 25.7 %collective-permute-start.49 = (bf16[512,256]{1,0:T(8,128)(2,1)S(1)}, bf16[512,256]{1,0:T(8,128)(2,1)S(1)}, u32[]{:S(2)}, u32[]{:S(2)}) collective-permute-start(bf16[512,256]{1,0:T(8,128)(2,1)S(1)} %get-tuple-element.585), channel_id=1, source_target_pairs={{0,8},{4,12},{8,0},{12,4},{16,24},{20,28},{24,16},{28,20},{1,9},{5... | collective-permute-start | bytes 786440 | tf_op jit(solution)/shard_map/ppermute | solution.py:17
  359.6 48.1 %collective-permute-start.52 = (bf16[512,2048]{1,0:T(8,128)(2,1)S(1)}, bf16[512,2048]{1,0:T(8,128)(2,1)S(1)}, u32[]{:S(2)}, u32[]{:S(2)}) collective-permute-start(bf16[512,2048]{1,0:T(8,128)(2,1)S(1)} %add_convert_fusion.1), channel_id=1, source_target_pairs={{0,2},{1,3},{2,0},{3,1},{4,6},{5,7},{6,4},{7,5},{8,10},{9,11},{10,... | collective-permute-start | bytes 6291464 | tf_op jit(solution)/shard_map/ppermute | solution.py:17
  360.5 47.2 %collective-permute-start.53 = (bf16[512,2048]{1,0:T(8,128)(2,1)S(1)}, bf16[512,2048]{1,0:T(8,128)(2,1)S(1)}, u32[]{:S(2)}, u32[]{:S(2)}) collective-permute-start(bf16[512,2048]{1,0:T(8,128)(2,1)S(1)} %out_block.6), channel_id=1, source_target_pairs={{0,1},{1,0},{2,3},{3,2},{4,5},{5,4},{6,7},{7,6},{8,9},{9,8},{10,11... | collective-permute-start | bytes 6291464 | tf_op jit(solution)/shard_map/ppermute | solution.py:17
  (109 other events, 1577.6 us)

commit v2 on v1

--- a/solution.py
+++ b/solution.py
@@ -398,7 +398,11 @@
 
     def halo(i):
         edge, other = state.pop(("edge", i)), state.pop(("other edge", i))
-        before = jnp.concatenate([lax.ppermute(edge[-1:], "seq", far), other[:-1]], 0)
+        if i % 2:
+            crossed = lax.ppermute(other[-1:], "seq", [(2 * k, 2 * (near + k)) for k in range(near)])
+        else:
+            crossed = lax.ppermute(edge[-1:], "seq", far)
+        before = jnp.concatenate([crossed, other[:-1]], 0)
         rows = jnp.where(odd == 1, other, before)
         rows = [lax.dynamic_index_in_dim(rows, place ^ o, 0, False) for o in range(near)]
         state["halo", i] = jnp.stack(rows)

time: 415 us -> 411 us (level)
  starting transfers between devices: 67.9 us -> 62.9 us
    ppermute x52, starting transfers between devices: 65 us -> 60.3 us  [swapped(): lax.ppermute(value, axis, [(i, i ^ bit) for i in range(lax.axis_size(axis...]
where the time goes in v2:
time: 411 us; the launch traced here: 407 us
  waiting for transfers between devices  215 us (52%)
  Pallas kernels  69.7 us (17%)
  starting transfers between devices  62.9 us (15%)
  local copies, waits for them, and re-layouts  30 us (7%)
  other arithmetic  23.2 us (6%)
    ppermute x52, waiting for transfers between devices, swapped(): lax.ppermute(value, axis, [(i, i ^ bit) for i in range(lax.axis_size(axis...  211 us
    ppermute x52, starting transfers between devices, swapped(): lax.ppermute(value, axis, [(i, i ^ bit) for i in range(lax.axis_size(axis...  60.3 us
    pallas_call x12, Pallas kernels, project(): pl.pallas_call(kernel, in_specs=[smem, smem] + [vmem] * (2 + len(flat)),...  45.4 us
    pallas_call x4, Pallas kernels, out_block(): pl.pallas_call(kernel, in_specs=[pl.BlockSpec(memory_space=pltpu.SMEM), v...  16.4 us
    unnamed x177, local copies, waits for them, and re-layouts  10.1 us
  transfers between devices with their start and end apart: 54, of which 25 were waited for; matrix products, arithmetic and copies ran while one was open for 10% of the time, Pallas kernels for 15%

profile of v2, /device:TPU:4, one launch (start us, length us, event | category | flops | bytes accessed | tf_op | source)
XLA Modules:
  0.0 406.8 jit_solution(1781345621917689744)
XLA Ops:
  4.3 6.8 %slice_bitcast_fusion = (bf16[3,512,1024]{2,1,0:T(8,128)(2,1)}, bf16[3,512,1024]{2,1,0:T(8,128)(2,1)}) fusion(bf16[1024,3,1024]{2,0,1:T(8,128)(2,1)} %param.9), kind=kLoop, calls=%fused_computation.5 | loop fusion | bytes 12582912 | tf_op jit(solution)/shard_map/transpose | solution.py:208
  15.8 3.8 fusion.2
  27.5 5.9 %collective-permute-done.4.refs_6_ = bf16[3,512,256]{2,1,0:T(8,128)(2,1)S(1)} collective-permute-done((bf16[3,512,256]{2,1,0:T(8,128)(2,1)}, bf16[3,512,256]{2,1,0:T(8,128)(2,1)S(1)}, u32[]{:S(2)}, u32[]{:S(2)}) %collective-permute-start.4) | collective-permute-done | bytes 786464 | tf_op jit(solution)/shard_map/ppermute | solution.py:17
  42.9 17.7 %collective-permute-done.10.refs_7_ = bf16[3,512,256]{2,1,0:T(8,128)(2,1)S(1)} collective-permute-done((bf16[3,512,256]{2,1,0:T(8,128)(2,1)S(1)}, bf16[3,512,256]{2,1,0:T(8,128)(2,1)S(1)}, u32[]{:S(2)}, u32[]{:S(2)}) %collective-permute-start.10) | collective-permute-done | bytes 786464 | tf_op jit(solution)/shard_map/ppermute | solution.py:17
  68.3 10.1 %collective-permute-done.11 = bf16[48,4096]{1,0:T(8,128)(2,1)S(1)} collective-permute-done((bf16[48,4096]{1,0:T(8,128)(2,1)S(1)}, bf16[48,4096]{1,0:T(8,128)(2,1)S(1)}, u32[]{:S(2)}, u32[]{:S(2)}) %collective-permute-start.11) | collective-permute-done | bytes 393248 | tf_op jit(solution)/shard_map/ppermute | solution.py:17
  78.4 5.5 %collective-permute-done.12 = bf16[48,4096]{1,0:T(8,128)(2,1)S(1)} collective-permute-done((bf16[48,4096]{1,0:T(8,128)(2,1)S(1)}, bf16[48,4096]{1,0:T(8,128)(2,1)S(1)}, u32[]{:S(2)}, u32[]{:S(2)}) %collective-permute-start.12) | collective-permute-done | bytes 393248 | tf_op jit(solution)/shard_map/ppermute | solution.py:17
  87.7 10.2 %collective-permute-done.15 = bf16[48,4096]{1,0:T(8,128)(2,1)S(1)} collective-permute-done((bf16[48,4096]{1,0:T(8,128)(2,1)S(1)}, bf16[48,4096]{1,0:T(8,128)(2,1)S(1)}, u32[]{:S(2)}, u32[]{:S(2)}) %collective-permute-start.15) | collective-permute-done | bytes 393248 | tf_op jit(solution)/shard_map/ppermute | solution.py:17
  109.0 5.1 %collective-permute-done.19 = bf16[32,4096]{1,0:T(8,128)(2,1)S(1)} collective-permute-done((bf16[32,4096]{1,0:T(8,128)(2,1)}, bf16[32,4096]{1,0:T(8,128)(2,1)S(1)}, u32[]{:S(2)}, u32[]{:S(2)}) %collective-permute-start.19) | collective-permute-done | bytes 262176 | tf_op jit(solution)/shard_map/ppermute | solution.py:17
  114.2 10.0 %collective-permute-done.18 = bf16[96,4096]{1,0:T(8,128)(2,1)} collective-permute-done((bf16[96,4096]{1,0:T(8,128)(2,1)}, bf16[96,4096]{1,0:T(8,128)(2,1)}, u32[]{:S(2)}, u32[]{:S(2)}) %collective-permute-start.18) | collective-permute-done | bytes 786464 | tf_op jit(solution)/shard_map/ppermute | solution.py:17
  125.7 4.9 %project.12 = bf16[384,768]{1,0:T(8,128)(2,1)S(1)} custom-call(s32[4]{0:T(128)S(1)} %get-tuple-element.619.order_ref, s32[4]{0:T(128)S(1)} %get-tuple-element.620.places_ref, bf16[192,4096]{1,0:T(8,128)(2,1)} %pad_maximum_fusion.refs_0_, bf16[192,4096]{1,0:T(8,128)(2,1)} %collective-permute-done.20.refs_1_, ...), custom_call_target="tpu_custom_call" | custom-call | flops 1 | bytes 1 | tf_op jit(solution)/shard_map/project/pallas_call | solution.py:54
  135.5 9.5 %collective-permute-done.23 = bf16[64,4096]{1,0:T(8,128)(2,1)S(1)} collective-permute-done((bf16[64,4096]{1,0:T(8,128)(2,1)S(1)}, bf16[64,4096]{1,0:T(8,128)(2,1)S(1)}, u32[]{:S(2)}, u32[]{:S(2)}) %collective-permute-start.23) | collective-permute-done | bytes 524320 | tf_op jit(solution)/shard_map/ppermute | solution.py:17
  148.6 14.9 %collective-permute-done.24 = bf16[384,768]{1,0:T(8,128)(2,1)S(1)} collective-permute-done((bf16[384,768]{1,0:T(8,128)(2,1)S(1)}, bf16[384,768]{1,0:T(8,128)(2,1)S(1)}, u32[]{:S(2)}, u32[]{:S(2)}) %collective-permute-start.24) | collective-permute-done | bytes 589856 | tf_op jit(solution)/shard_map/ppermute | solution.py:17
  168.3 16.2 %collective-permute-done.28 = bf16[48,4096]{1,0:T(8,128)(2,1)S(1)} collective-permute-done((bf16[48,4096]{1,0:T(8,128)(2,1)S(1)}, bf16[48,4096]{1,0:T(8,128)(2,1)S(1)}, u32[]{:S(2)}, u32[]{:S(2)}) %collective-permute-start.28) | collective-permute-done | bytes 393248 | tf_op jit(solution)/shard_map/ppermute | solution.py:17
  187.5 8.4 %collective-permute-done.29 = bf16[384,768]{1,0:T(8,128)(2,1)S(1)} collective-permute-done((bf16[384,768]{1,0:T(8,128)(2,1)S(1)}, bf16[384,768]{1,0:T(8,128)(2,1)S(1)}, u32[]{:S(2)}, u32[]{:S(2)}) %collective-permute-start.29) | collective-permute-done | bytes 589856 | tf_op jit(solution)/shard_map/ppermute | solution.py:17
  201.5 8.3 %collective-permute-done.34 = bf16[32,4096]{1,0:T(8,128)(2,1)S(1)} collective-permute-done((bf16[32,4096]{1,0:T(8,128)(2,1)S(1)}, bf16[32,4096]{1,0:T(8,128)(2,1)S(1)}, u32[]{:S(2)}, u32[]{:S(2)}) %collective-permute-start.34) | collective-permute-done | bytes 262176 | tf_op jit(solution)/shard_map/ppermute | solution.py:17
  210.7 9.4 %collective-permute-done.33 = bf16[48,4096]{1,0:T(8,128)(2,1)S(1)} collective-permute-done((bf16[48,4096]{1,0:T(8,128)(2,1)S(1)}, bf16[48,4096]{1,0:T(8,128)(2,1)S(1)}, u32[]{:S(2)}, u32[]{:S(2)}) %collective-permute-start.33) | collective-permute-done | bytes 393248 | tf_op jit(solution)/shard_map/ppermute | solution.py:17
  222.0 4.7 %project.15 = bf16[384,768]{1,0:T(8,128)(2,1)S(1)} custom-call(s32[4]{0:T(128)S(1)} %get-tuple-element.619.order_ref, s32[4]{0:T(128)S(1)} %get-tuple-element.620.places_ref, bf16[192,4096]{1,0:T(8,128)(2,1)} %pad_maximum_fusion.refs_0_, bf16[192,4096]{1,0:T(8,128)(2,1)} %collective-permute-done.20.refs_1_, ...), custom_call_target="tpu_custom_call" | custom-call | flops 1 | bytes 1 | tf_op jit(solution)/shard_map/project/pallas_call | solution.py:54
  231.5 9.5 %collective-permute-done.37 = bf16[96,4096]{1,0:T(8,128)(2,1)S(1)} collective-permute-done((bf16[96,4096]{1,0:T(8,128)(2,1)S(1)}, bf16[96,4096]{1,0:T(8,128)(2,1)S(1)}, u32[]{:S(2)}, u32[]{:S(2)}) %collective-permute-start.37) | collective-permute-done | bytes 786464 | tf_op jit(solution)/shard_map/ppermute | solution.py:17
  250.0 5.6 %collective-permute-done.38 = bf16[384,768]{1,0:T(8,128)(2,1)S(1)} collective-permute-done((bf16[384,768]{1,0:T(8,128)(2,1)S(1)}, bf16[384,768]{1,0:T(8,128)(2,1)S(1)}, u32[]{:S(2)}, u32[]{:S(2)}) %collective-permute-start.38) | collective-permute-done | bytes 589856 | tf_op jit(solution)/shard_map/ppermute | solution.py:17
  272.1 4.9 %project.21 = bf16[384,768]{1,0:T(8,128)(2,1)S(1)} custom-call(s32[4]{0:T(128)S(1)} %get-tuple-element.619.order_ref, s32[4]{0:T(128)S(1)} %get-tuple-element.620.places_ref, bf16[192,4096]{1,0:T(8,128)(2,1)} %pad_maximum_fusion.3.refs_0_, bf16[192,4096]{1,0:T(8,128)(2,1)} %collective-permute-done.42.refs_1_, ...), custom_call_target="tpu_custom_call" | custom-call | flops 1 | bytes 1 | tf_op jit(solution)/shard_map/project/pallas_call | solution.py:54
  277.0 4.9 %project.20 = bf16[384,768]{1,0:T(8,128)(2,1)S(1)} custom-call(s32[4]{0:T(128)S(1)} %get-tuple-element.619.order_ref, s32[4]{0:T(128)S(1)} %get-tuple-element.620.places_ref, bf16[192,4096]{1,0:T(8,128)(2,1)} %pad_maximum_fusion.3.refs_0_, bf16[192,4096]{1,0:T(8,128)(2,1)} %collective-permute-done.42.refs_1_, ...), custom_call_target="tpu_custom_call" | custom-call | flops 1 | bytes 1 | tf_op jit(solution)/shard_map/project/pallas_call | solution.py:54
  282.8 6.6 %collective-permute-done.41 = bf16[384,768]{1,0:T(8,128)(2,1)S(1)} collective-permute-done((bf16[384,768]{1,0:T(8,128)(2,1)}, bf16[384,768]{1,0:T(8,128)(2,1)S(1)}, u32[]{:S(2)}, u32[]{:S(2)}) %collective-permute-start.41) | collective-permute-done | bytes 589856 | tf_op jit(solution)/shard_map/ppermute | solution.py:17
  296.0 3.9 collective-permute-done.46
  305.0 3.8 gate.2
  308.9 14.3 %collective-permute-start.49 = (bf16[512,256]{1,0:T(8,128)(2,1)S(1)}, bf16[512,256]{1,0:T(8,128)(2,1)S(1)}, u32[]{:S(2)}, u32[]{:S(2)}) collective-permute-start(bf16[512,256]{1,0:T(8,128)(2,1)S(1)} %get-tuple-element.583), channel_id=1, source_target_pairs={{0,8},{4,12},{8,0},{12,4},{16,24},{20,28},{24,16},{28,20},{1,9},{5... | collective-permute-start | bytes 786440 | tf_op jit(solution)/shard_map/ppermute | solution.py:17
  329.8 4.1 %gate.3 = bf16[2,512,256]{2,1,0:T(8,128)(2,1)S(1)} custom-call(bf16[2,144,768]{2,1,0:T(8,128)(2,1)S(1)} %pad_maximum_fusion.18.refs_0_, bf16[2,128,768]{2,1,0:T(8,128)(2,1)S(1)} %bitcast.118, bf16[2,128,768]{2,1,0:T(8,128)(2,1)S(1)} %bitcast.123, bf16[2,192,768]{2,1,0:T(8,128)(2,1)S(1)} %bitcast.112, bf16[2,192,768]{2,1,0:T(8,128)(2,1)S(1)} %bitcast.121, ...), custom_call_target="tpu_custom_call" | custom-call | flops 1 | bytes 1 | tf_op jit(solution)/shard_map/gate/pallas_call | solution.py:111
  335.9 5.8 %collective-permute-done.50 = bf16[512,256]{1,0:T(8,128)(2,1)S(1)} collective-permute-done((bf16[512,256]{1,0:T(8,128)(2,1)S(1)}, bf16[512,256]{1,0:T(8,128)(2,1)S(1)}, u32[]{:S(2)}, u32[]{:S(2)}) %collective-permute-start.50) | collective-permute-done | bytes 262176 | tf_op jit(solution)/shard_map/ppermute | solution.py:17
  341.8 4.1 %out_block.5 = bf16[512,2048]{1,0:T(8,128)(2,1)S(1)} custom-call(s32[1]{0:T(128)} %bitcast.62.block_ref, bf16[512,1024]{1,0:T(8,128)(2,1)S(1)} %maximum_dynamic-update-slice_fusion.1.gating_ref, bf16[1024,8192]{1,0:T(8,128)(2,1)} %w_ref.7), custom_call_target="tpu_custom_call" | custom-call | flops 1 | bytes 1 | tf_op jit(solution)/shard_map/out_block/pallas_call | solution.py:150
  346.0 4.1 %out_block.6 = bf16[512,2048]{1,0:T(8,128)(2,1)S(1)} custom-call(s32[1]{0:T(128)} %bitcast.39.block_ref, bf16[512,1024]{1,0:T(8,128)(2,1)S(1)} %maximum_dynamic-update-slice_fusion.1.gating_ref, bf16[1024,8192]{1,0:T(8,128)(2,1)} %w_ref.7), custom_call_target="tpu_custom_call" | custom-call | flops 1 | bytes 1 | tf_op jit(solution)/shard_map/out_block/pallas_call | solution.py:150
  350.1 4.1 %out_block.4 = bf16[512,2048]{1,0:T(8,128)(2,1)S(1)} custom-call(s32[1]{0:T(128)} %bitcast.40.block_ref, bf16[512,1024]{1,0:T(8,128)(2,1)S(1)} %maximum_dynamic-update-slice_fusion.1.gating_ref, bf16[1024,8192]{1,0:T(8,128)(2,1)} %w_ref.7), custom_call_target="tpu_custom_call" | custom-call | flops 1 | bytes 1 | tf_op jit(solution)/shard_map/out_block/pallas_call | solution.py:150
  356.3 4.1 %out_block.7 = bf16[512,2048]{1,0:T(8,128)(2,1)S(1)} custom-call(s32[1]{0:T(128)} %bitcast.block_ref, bf16[512,1024]{1,0:T(8,128)(2,1)S(1)} %maximum_dynamic-update-slice_fusion.1.gating_ref, bf16[1024,8192]{1,0:T(8,128)(2,1)} %w_ref.7), custom_call_target="tpu_custom_call" | custom-call | flops 1 | bytes 1 | tf_op jit(solution)/shard_map/out_block/pallas_call | solution.py:150
  360.4 42.9 %collective-permute-done.52 = bf16[512,2048]{1,0:T(8,128)(2,1)S(1)} collective-permute-done((bf16[512,2048]{1,0:T(8,128)(2,1)S(1)}, bf16[512,2048]{1,0:T(8,128)(2,1)S(1)}, u32[]{:S(2)}, u32[]{:S(2)}) %collective-permute-start.52) | collective-permute-done | bytes 2097184 | tf_op jit(solution)/shard_map/ppermute | solution.py:17
  (351 shorter events, 130.7 us)
Async XLA Ops:
  2.5 23.0 %collective-permute-start.2 = (bf16[48,2048]{1,0:T(8,128)(2,1)}, bf16[48,2048]{1,0:T(8,128)(2,1)}, u32[]{:S(2)}, u32[]{:S(2)}) collective-permute-start(bf16[48,2048]{1,0:T(8,128)(2,1)} %get-tuple-element.565), channel_id=1, source_target_pairs={{0,3},{1,2},{2,1},{3,0},{4,7},{5,6},{6,5},{7,4},{8,11},{9,10},{10,... | collective-permute-start | bytes 589832 | tf_op jit(solution)/shard_map/ppermute | solution.py:17
  3.4 22.2 %collective-permute-start.1 = (bf16[48,2048]{1,0:T(8,128)(2,1)}, bf16[48,2048]{1,0:T(8,128)(2,1)}, u32[]{:S(2)}, u32[]{:S(2)}) collective-permute-start(bf16[48,2048]{1,0:T(8,128)(2,1)} %get-tuple-element.566), channel_id=1, source_target_pairs={{0,2},{1,3},{2,0},{3,1},{4,6},{5,7},{6,4},{7,5},{8,10},{9,11},{10,... | collective-permute-start | bytes 589832 | tf_op jit(solution)/shard_map/ppermute | solution.py:17
  4.0 23.1 %collective-permute-start = (bf16[48,2048]{1,0:T(8,128)(2,1)}, bf16[48,2048]{1,0:T(8,128)(2,1)}, u32[]{:S(2)}, u32[]{:S(2)}) collective-permute-start(bf16[48,2048]{1,0:T(8,128)(2,1)} %get-tuple-element.567), channel_id=1, source_target_pairs={{0,1},{1,0},{2,3},{3,2},{4,5},{5,4},{6,7},{7,6},{8,9},{9,8},{10,11... | collective-permute-start | bytes 589832 | tf_op jit(solution)/shard_map/ppermute | solution.py:17
  33.4 27.2 %collective-permute-start.10 = (bf16[3,512,256]{2,1,0:T(8,128)(2,1)S(1)}, bf16[3,512,256]{2,1,0:T(8,128)(2,1)S(1)}, u32[]{:S(2)}, u32[]{:S(2)}) collective-permute-start(bf16[3,512,256]{2,1,0:T(8,128)(2,1)S(1)} %get-tuple-element.555), channel_id=1, source_target_pairs={{0,8},{4,12},{8,0},{12,4},{16,24},{20,28},{24,16},{28,20},{1,9},{5... | collective-permute-start | bytes 2359304 | tf_op jit(solution)/shard_map/ppermute | solution.py:17
  35.0 25.6 %collective-permute-start.9 = (bf16[3,512,256]{2,1,0:T(8,128)(2,1)S(1)}, bf16[3,512,256]{2,1,0:T(8,128)(2,1)S(1)}, u32[]{:S(2)}, u32[]{:S(2)}) collective-permute-start(bf16[3,512,256]{2,1,0:T(8,128)(2,1)S(1)} %get-tuple-element.519.refs_3_), channel_id=1, source_target_pairs={{0,4},{4,0},{8,12},{12,8},{16,20},{20,16},{24,28},{28,24},{1,5},{5... | collective-permute-start | bytes 2359304 | tf_op jit(solution)/shard_map/ppermute | solution.py:17
  39.5 21.2 %collective-permute-start.5 = (bf16[48,4096]{1,0:T(8,128)(2,1)S(1)}, bf16[48,4096]{1,0:T(8,128)(2,1)S(1)}, u32[]{:S(2)}, u32[]{:S(2)}) collective-permute-start(bf16[48,4096]{1,0:T(8,128)(2,1)S(1)} %pad_maximum_fusion.20), channel_id=1, source_target_pairs={{0,16},{4,20},{8,24},{12,28},{16,0},{20,4},{24,8},{28,12},{1,17},{... | collective-permute-start | bytes 1179656 | tf_op jit(solution)/shard_map/ppermute | solution.py:17
  103.8 21.8 %collective-permute-start.20 = (bf16[192,4096]{1,0:T(8,128)(2,1)}, bf16[192,4096]{1,0:T(8,128)(2,1)}, u32[]{:S(2)}, u32[]{:S(2)}) collective-permute-start(bf16[192,4096]{1,0:T(8,128)(2,1)} %pad_maximum_fusion.refs_0_), channel_id=1, source_target_pairs={{0,1},{1,0},{2,3},{3,2},{4,5},{5,4},{6,7},{7,6},{8,9},{9,8},{10,11... | collective-permute-start | bytes 4718600 | tf_op jit(solution)/shard_map/ppermute | solution.py:17
  103.8 20.3 %collective-permute-start.18 = (bf16[96,4096]{1,0:T(8,128)(2,1)}, bf16[96,4096]{1,0:T(8,128)(2,1)}, u32[]{:S(2)}, u32[]{:S(2)}) collective-permute-start(bf16[96,4096]{1,0:T(8,128)(2,1)} %pad_maximum_fusion.9), channel_id=1, source_target_pairs={{0,2},{1,3},{2,0},{3,1},{4,6},{5,7},{6,4},{7,5},{8,10},{9,11},{10,... | collective-permute-start | bytes 2359304 | tf_op jit(solution)/shard_map/ppermute | solution.py:17
  108.0 22.6 %collective-permute-start.21 = (bf16[3,512,256]{2,1,0:T(8,128)(2,1)S(1)}, bf16[3,512,256]{2,1,0:T(8,128)(2,1)S(1)}, u32[]{:S(2)}, u32[]{:S(2)}) collective-permute-start(bf16[3,512,256]{2,1,0:T(8,128)(2,1)S(1)} %get-tuple-element.554), channel_id=1, source_target_pairs={{0,8},{4,12},{8,0},{12,4},{16,24},{20,28},{24,16},{28,20},{1,9},{5... | collective-permute-start | bytes 2359304 | tf_op jit(solution)/shard_map/ppermute | solution.py:17
  108.4 22.2 %collective-permute-start.22 = (bf16[3,512,256]{2,1,0:T(8,128)(2,1)S(1)}, bf16[3,512,256]{2,1,0:T(8,128)(2,1)S(1)}, u32[]{:S(2)}, u32[]{:S(2)}) collective-permute-start(bf16[3,512,256]{2,1,0:T(8,128)(2,1)S(1)} %get-tuple-element.526.refs_2_), channel_id=1, source_target_pairs={{0,4},{4,0},{8,12},{12,8},{16,20},{20,16},{24,28},{28,24},{1,5},{5... | collective-permute-start | bytes 2359304 | tf_op jit(solution)/shard_map/ppermute | solution.py:17
  131.9 32.3 %collective-permute-start.26 = (bf16[3,512,256]{2,1,0:T(8,128)(2,1)S(1)}, bf16[3,512,256]{2,1,0:T(8,128)(2,1)S(1)}, u32[]{:S(2)}, u32[]{:S(2)}) collective-permute-start(bf16[3,512,256]{2,1,0:T(8,128)(2,1)S(1)} %get-tuple-element.552), channel_id=1, source_target_pairs={{0,8},{4,12},{8,0},{12,4},{16,24},{20,28},{24,16},{28,20},{1,9},{5... | collective-permute-start | bytes 2359304 | tf_op jit(solution)/shard_map/ppermute | solution.py:17
  133.7 30.6 %collective-permute-start.27 = (bf16[3,512,256]{2,1,0:T(8,128)(2,1)S(1)}, bf16[3,512,256]{2,1,0:T(8,128)(2,1)S(1)}, u32[]{:S(2)}, u32[]{:S(2)}) collective-permute-start(bf16[3,512,256]{2,1,0:T(8,128)(2,1)S(1)} %get-tuple-element.527.refs_3_), channel_id=1, source_target_pairs={{0,4},{4,0},{8,12},{12,8},{16,20},{20,16},{24,28},{28,24},{1,5},{5... | collective-permute-start | bytes 2359304 | tf_op jit(solution)/shard_map/ppermute | solution.py:17
  134.2 29.3 %collective-permute-start.24 = (bf16[384,768]{1,0:T(8,128)(2,1)S(1)}, bf16[384,768]{1,0:T(8,128)(2,1)S(1)}, u32[]{:S(2)}, u32[]{:S(2)}) collective-permute-start(bf16[384,768]{1,0:T(8,128)(2,1)S(1)} %project.12), channel_id=1, source_target_pairs={{0,16},{4,20},{8,24},{12,28},{16,0},{20,4},{24,8},{28,12},{1,17},{... | collective-permute-start | bytes 1769480 | tf_op jit(solution)/shard_map/ppermute | solution.py:17
  164.3 20.3 %collective-permute-start.30 = (bf16[128,4096]{1,0:T(8,128)(2,1)S(1)}, bf16[128,4096]{1,0:T(8,128)(2,1)S(1)}, u32[]{:S(2)}, u32[]{:S(2)}) collective-permute-start(bf16[128,4096]{1,0:T(8,128)(2,1)S(1)} %pad_maximum_fusion.4.refs_0_), channel_id=1, source_target_pairs={{0,1},{1,0},{2,3},{3,2},{4,5},{5,4},{6,7},{7,6},{8,9},{9,8},{10,11... | collective-permute-start | bytes 3145736 | tf_op jit(solution)/shard_map/ppermute | solution.py:17
  164.3 20.2 %collective-permute-start.28 = (bf16[48,4096]{1,0:T(8,128)(2,1)S(1)}, bf16[48,4096]{1,0:T(8,128)(2,1)S(1)}, u32[]{:S(2)}, u32[]{:S(2)}) collective-permute-start(bf16[48,4096]{1,0:T(8,128)(2,1)S(1)} %copy-done.75), channel_id=1, source_target_pairs={{0,8},{4,12},{8,0},{12,4},{16,24},{20,28},{24,16},{28,20},{1,9},{5... | collective-permute-start | bytes 1179656 | tf_op jit(solution)/shard_map/ppermute | solution.py:17
  166.7 29.2 %collective-permute-start.31 = (bf16[3,512,256]{2,1,0:T(8,128)(2,1)S(1)}, bf16[3,512,256]{2,1,0:T(8,128)(2,1)S(1)}, u32[]{:S(2)}, u32[]{:S(2)}) collective-permute-start(bf16[3,512,256]{2,1,0:T(8,128)(2,1)S(1)} %collective-permute-done.21.refs_6_), channel_id=1, source_target_pairs={{0,4},{4,0},{8,12},{12,8},{16,20},{20,16},{24,28},{28,24},{1,5},{5... | collective-permute-start | bytes 2359304 | tf_op jit(solution)/shard_map/ppermute | solution.py:17
  167.2 28.7 %collective-permute-start.29 = (bf16[384,768]{1,0:T(8,128)(2,1)S(1)}, bf16[384,768]{1,0:T(8,128)(2,1)S(1)}, u32[]{:S(2)}, u32[]{:S(2)}) collective-permute-start(bf16[384,768]{1,0:T(8,128)(2,1)S(1)} %project.13), channel_id=1, source_target_pairs={{0,16},{4,20},{8,24},{12,28},{16,0},{20,4},{24,8},{28,12},{1,17},{... | collective-permute-start | bytes 1769480 | tf_op jit(solution)/shard_map/ppermute | solution.py:17
  196.0 24.3 %collective-permute-start.35 = (bf16[256,768]{1,0:T(8,128)(2,1)S(1)}, bf16[256,768]{1,0:T(8,128)(2,1)S(1)}, u32[]{:S(2)}, u32[]{:S(2)}) collective-permute-start(bf16[256,768]{1,0:T(8,128)(2,1)S(1)} %project.14), channel_id=1, source_target_pairs={{0,16},{4,20},{8,24},{12,28},{16,0},{20,4},{24,8},{28,12},{1,17},{... | collective-permute-start | bytes 1179656 | tf_op jit(solution)/shard_map/ppermute | solution.py:17
  199.0 21.1 %collective-permute-start.33 = (bf16[48,4096]{1,0:T(8,128)(2,1)S(1)}, bf16[48,4096]{1,0:T(8,128)(2,1)S(1)}, u32[]{:S(2)}, u32[]{:S(2)}) collective-permute-start(bf16[48,4096]{1,0:T(8,128)(2,1)S(1)} %copy-done.76), channel_id=1, source_target_pairs={{0,8},{4,12},{8,0},{12,4},{16,24},{20,28},{24,16},{28,20},{1,9},{5... | collective-permute-start | bytes 1179656 | tf_op jit(solution)/shard_map/ppermute | solution.py:17
  199.1 21.1 %collective-permute-start.32 = (bf16[96,4096]{1,0:T(8,128)(2,1)S(1)}, bf16[96,4096]{1,0:T(8,128)(2,1)S(1)}, u32[]{:S(2)}, u32[]{:S(2)}) collective-permute-start(bf16[96,4096]{1,0:T(8,128)(2,1)S(1)} %pad_maximum_fusion.10), channel_id=1, source_target_pairs={{0,2},{1,3},{2,0},{3,1},{4,6},{5,7},{6,4},{7,5},{8,10},{9,11},{10,... | collective-permute-start | bytes 2359304 | tf_op jit(solution)/shard_map/ppermute | solution.py:17
  200.0 21.1 %collective-permute-start.36 = (bf16[3,512,256]{2,1,0:T(8,128)(2,1)S(1)}, bf16[3,512,256]{2,1,0:T(8,128)(2,1)S(1)}, u32[]{:S(2)}, u32[]{:S(2)}) collective-permute-start(bf16[3,512,256]{2,1,0:T(8,128)(2,1)S(1)} %collective-permute-done.26.refs_7_), channel_id=1, source_target_pairs={{0,4},{4,0},{8,12},{12,8},{16,20},{20,16},{24,28},{28,24},{1,5},{5... | collective-permute-start | bytes 2359304 | tf_op jit(solution)/shard_map/ppermute | solution.py:17
  221.1 21.3 %collective-permute-start.39 = (bf16[192,4096]{1,0:T(8,128)(2,1)S(1)}, bf16[192,4096]{1,0:T(8,128)(2,1)S(1)}, u32[]{:S(2)}, u32[]{:S(2)}) collective-permute-start(bf16[192,4096]{1,0:T(8,128)(2,1)S(1)} %pad_maximum_fusion.2.refs_0_), channel_id=1, source_target_pairs={{0,1},{1,0},{2,3},{3,2},{4,5},{5,4},{6,7},{7,6},{8,9},{9,8},{10,11... | collective-permute-start | bytes 4718600 | tf_op jit(solution)/shard_map/ppermute | solution.py:17
  221.1 20.0 %collective-permute-start.37 = (bf16[96,4096]{1,0:T(8,128)(2,1)S(1)}, bf16[96,4096]{1,0:T(8,128)(2,1)S(1)}, u32[]{:S(2)}, u32[]{:S(2)}) collective-permute-start(bf16[96,4096]{1,0:T(8,128)(2,1)S(1)} %pad_maximum_fusion.11), channel_id=1, source_target_pairs={{0,2},{1,3},{2,0},{3,1},{4,6},{5,7},{6,4},{7,5},{8,10},{9,11},{10,... | collective-permute-start | bytes 2359304 | tf_op jit(solution)/shard_map/ppermute | solution.py:17
  226.7 28.8 %collective-permute-start.38 = (bf16[384,768]{1,0:T(8,128)(2,1)S(1)}, bf16[384,768]{1,0:T(8,128)(2,1)S(1)}, u32[]{:S(2)}, u32[]{:S(2)}) collective-permute-start(bf16[384,768]{1,0:T(8,128)(2,1)S(1)} %project.15), channel_id=1, source_target_pairs={{0,16},{4,20},{8,24},{12,28},{16,0},{20,4},{24,8},{28,12},{1,17},{... | collective-permute-start | bytes 1769480 | tf_op jit(solution)/shard_map/ppermute | solution.py:17
  259.2 23.6 %collective-permute-start.43 = (bf16[2,144,768]{2,1,0:T(8,128)(2,1)S(1)}, bf16[2,144,768]{2,1,0:T(8,128)(2,1)S(1)}, u32[]{:S(2)}, u32[]{:S(2)}) collective-permute-start(bf16[2,144,768]{2,1,0:T(8,128)(2,1)S(1)} %pad_maximum_fusion.15), channel_id=1, source_target_pairs={{0,4},{4,0},{8,12},{12,8},{16,20},{20,16},{24,28},{28,24},{1,5},{5... | collective-permute-start | bytes 1327112 | tf_op jit(solution)/shard_map/ppermute | solution.py:17
  260.8 28.7 %collective-permute-start.41 = (bf16[384,768]{1,0:T(8,128)(2,1)}, bf16[384,768]{1,0:T(8,128)(2,1)S(1)}, u32[]{:S(2)}, u32[]{:S(2)}) collective-permute-start(bf16[384,768]{1,0:T(8,128)(2,1)} %copy-done.66), channel_id=1, source_target_pairs={{0,16},{4,20},{8,24},{12,28},{16,0},{20,4},{24,8},{28,12},{1,17},{... | collective-permute-start | bytes 1769480 | tf_op jit(solution)/shard_map/ppermute | solution.py:17
  262.3 20.5 %collective-permute-start.44 = (bf16[2,144,768]{2,1,0:T(8,128)(2,1)S(1)}, bf16[2,144,768]{2,1,0:T(8,128)(2,1)S(1)}, u32[]{:S(2)}, u32[]{:S(2)}) collective-permute-start(bf16[2,144,768]{2,1,0:T(8,128)(2,1)S(1)} %pad_maximum_fusion.16), channel_id=1, source_target_pairs={{0,4},{4,0},{8,12},{12,8},{16,20},{20,16},{24,28},{28,24},{1,5},{5... | collective-permute-start | bytes 1327112 | tf_op jit(solution)/shard_map/ppermute | solution.py:17
  294.2 33.0 %collective-permute-start.45 = (bf16[256,768]{1,0:T(8,128)(2,1)}, bf16[256,768]{1,0:T(8,128)(2,1)S(1)}, u32[]{:S(2)}, u32[]{:S(2)}) collective-permute-start(bf16[256,768]{1,0:T(8,128)(2,1)} %copy-done.67), channel_id=1, source_target_pairs={{0,16},{4,20},{8,24},{12,28},{16,0},{20,4},{24,8},{28,12},{1,17},{... | collective-permute-start | bytes 1179656 | tf_op jit(solution)/shard_map/ppermute | solution.py:17
  295.4 27.9 %collective-permute-start.47 = (bf16[1,144,768]{2,1,0:T(8,128)(2,1)S(1)}, bf16[1,144,768]{2,1,0:T(8,128)(2,1)S(1)}, u32[]{:S(2)}, u32[]{:S(2)}) collective-permute-start(bf16[1,144,768]{2,1,0:T(8,128)(2,1)S(1)} %get-tuple-element.591), channel_id=1, source_target_pairs={{0,16},{8,24},{1,17},{9,25},{2,18},{10,26},{3,19},{11,27}} | collective-permute-start | bytes 663560 | tf_op jit(solution)/shard_map/ppermute | solution.py:402
  308.9 20.9 %collective-permute-start.49 = (bf16[512,256]{1,0:T(8,128)(2,1)S(1)}, bf16[512,256]{1,0:T(8,128)(2,1)S(1)}, u32[]{:S(2)}, u32[]{:S(2)}) collective-permute-start(bf16[512,256]{1,0:T(8,128)(2,1)S(1)} %get-tuple-element.583), channel_id=1, source_target_pairs={{0,8},{4,12},{8,0},{12,4},{16,24},{20,28},{24,16},{28,20},{1,9},{5... | collective-permute-start | bytes 786440 | tf_op jit(solution)/shard_map/ppermute | solution.py:17
  355.1 48.1 %collective-permute-start.52 = (bf16[512,2048]{1,0:T(8,128)(2,1)S(1)}, bf16[512,2048]{1,0:T(8,128)(2,1)S(1)}, u32[]{:S(2)}, u32[]{:S(2)}) collective-permute-start(bf16[512,2048]{1,0:T(8,128)(2,1)S(1)} %add_convert_fusion.1), channel_id=1, source_target_pairs={{0,2},{1,3},{2,0},{3,1},{4,6},{5,7},{6,4},{7,5},{8,10},{9,11},{10,... | collective-permute-start | bytes 6291464 | tf_op jit(solution)/shard_map/ppermute | solution.py:17
  356.0 47.2 %collective-permute-start.53 = (bf16[512,2048]{1,0:T(8,128)(2,1)S(1)}, bf16[512,2048]{1,0:T(8,128)(2,1)S(1)}, u32[]{:S(2)}, u32[]{:S(2)}) collective-permute-start(bf16[512,2048]{1,0:T(8,128)(2,1)S(1)} %out_block.6), channel_id=1, source_target_pairs={{0,1},{1,0},{2,3},{3,2},{4,5},{5,4},{6,7},{7,6},{8,9},{9,8},{10,11... | collective-permute-start | bytes 6291464 | tf_op jit(solution)/shard_map/ppermute | solution.py:17
  (108 other events, 1549.5 us)

commit v3 on v1

--- a/solution.py
+++ b/solution.py
@@ -373,7 +373,6 @@
     send(0, 2)
     across("kept", 0)
     near_rows("kept", 1)
-    near_rows("kept", 2)
     pair_near_w(1, 1)
     step()
     partial(1, 0)
@@ -381,10 +380,10 @@
     partial(1, 1)
     beside("kept", 0)
     across("kept", 1)
+    near_rows("kept", 2)
     own(0, 0)
     own(1, 0)
     step()
-    far = [(2 * i + 1, 2 * (near + i)) for i in range(near)]
 
     def term(kind, i, j):
         value = state[kind, i, j]
@@ -398,7 +397,17 @@
 
     def halo(i):
         edge, other = state.pop(("edge", i)), state.pop(("other edge", i))
-        before = jnp.concatenate([lax.ppermute(edge[-1:], "seq", far), other[:-1]], 0)
+        pairs = [
+            ((2 * k + 1 - c % 2) * ranks + c, 2 * (near + k) * ranks + c)
+            for k in range(near)
+            for c in range(ranks)
+        ]
+        leaving = jnp.where(odd == 1, edge[-1], other[-1])
+        packed = jnp.concatenate([leaving[:, width : 2 * width], leaving[:, 2 * width :], leaving[-16:, :width]], 0)
+        packed = lax.ppermute(packed, ("seq", "chan"), pairs)
+        first = jnp.concatenate([jnp.zeros((EDGE - 16, width), jnp.bfloat16), packed[2 * EDGE :]], 0)
+        crossed = jnp.concatenate([first, packed[:EDGE], packed[EDGE : 2 * EDGE]], 1)[None]
+        before = jnp.concatenate([crossed, other[:-1]], 0)
         rows = jnp.where(odd == 1, other, before)
         rows = [lax.dynamic_index_in_dim(rows, place ^ o, 0, False) for o in range(near)]
         state["halo", i] = jnp.stack(rows)

time: 415 us -> 407 us (0.981); the launches traced: 411 us -> 399 us
  local copies, waits for them, and re-layouts: 30.8 us -> 24.6 us
    ppermute x52, waiting for transfers between devices: 211 us -> 206 us  [swapped(): lax.ppermute(value, axis, [(i, i ^ bit) for i in range(lax.axis_size(axis...]
    ppermute x2, waiting for transfers between devices: 2.42 us -> 7.31 us  [halo(): packed = lax.ppermute(packed, ('seq', 'chan'), pairs)]
    ppermute x52, starting transfers between devices: 65 us -> 60.6 us  [swapped(): lax.ppermute(value, axis, [(i, i ^ bit) for i in range(lax.axis_size(axis...]
    unnamed x177 -> x131, local copies, waits for them, and re-layouts: 11.2 us -> 7.66 us
  transfers between devices with their start and end apart: 54 -> 54, of which waited for: 25 -> 28; matrix products, arithmetic and copies ran while one was open for 10% -> 9% of each run, Pallas kernels for 15% -> 15%
where the time goes in v3:
time: 407 us; the launch traced here: 399 us
  waiting for transfers between devices  213 us (52%)
  Pallas kernels  68.1 us (17%)
  starting transfers between devices  66 us (16%)
  local copies, waits for them, and re-layouts  24.6 us (6%)
  other arithmetic  21.4 us (5%)
    ppermute x52, waiting for transfers between devices, swapped(): lax.ppermute(value, axis, [(i, i ^ bit) for i in range(lax.axis_size(axis...  206 us
    ppermute x52, starting transfers between devices, swapped(): lax.ppermute(value, axis, [(i, i ^ bit) for i in range(lax.axis_size(axis...  60.6 us
    pallas_call x12, Pallas kernels, project(): pl.pallas_call(kernel, in_specs=[smem, smem] + [vmem] * (2 + len(flat)),...  43.7 us
    pallas_call x4, Pallas kernels, out_block(): pl.pallas_call(kernel, in_specs=[pl.BlockSpec(memory_space=pltpu.SMEM), v...  16.4 us
  transfers between devices with their start and end apart: 54, of which 28 were waited for; matrix products, arithmetic and copies ran while one was open for 9% of the time, Pallas kernels for 15%

profile of v3, /device:TPU:4, one launch (start us, length us, event | category | flops | bytes accessed | tf_op | source)
XLA Modules:
  0.0 398.9 jit_solution(17075628245902699671)
XLA Ops:
  4.4 6.8 %slice_bitcast_fusion = (bf16[3,512,1024]{2,1,0:T(8,128)(2,1)}, bf16[3,512,1024]{2,1,0:T(8,128)(2,1)}) fusion(bf16[1024,3,1024]{2,0,1:T(8,128)(2,1)} %param.9), kind=kLoop, calls=%fused_computation.5 | loop fusion | bytes 12582912 | tf_op jit(solution)/shard_map/transpose | solution.py:208
  27.5 6.0 %collective-permute-done.4.refs_6_ = bf16[3,512,256]{2,1,0:T(8,128)(2,1)S(1)} collective-permute-done((bf16[3,512,256]{2,1,0:T(8,128)(2,1)}, bf16[3,512,256]{2,1,0:T(8,128)(2,1)S(1)}, u32[]{:S(2)}, u32[]{:S(2)}) %collective-permute-start.4) | collective-permute-done | bytes 786464 | tf_op jit(solution)/shard_map/ppermute | solution.py:17
  42.9 17.7 %collective-permute-done.10.refs_7_ = bf16[3,512,256]{2,1,0:T(8,128)(2,1)S(1)} collective-permute-done((bf16[3,512,256]{2,1,0:T(8,128)(2,1)S(1)}, bf16[3,512,256]{2,1,0:T(8,128)(2,1)S(1)}, u32[]{:S(2)}, u32[]{:S(2)}) %collective-permute-start.10) | collective-permute-done | bytes 786464 | tf_op jit(solution)/shard_map/ppermute | solution.py:17
  68.3 10.1 %collective-permute-done.11 = bf16[48,4096]{1,0:T(8,128)(2,1)S(1)} collective-permute-done((bf16[48,4096]{1,0:T(8,128)(2,1)S(1)}, bf16[48,4096]{1,0:T(8,128)(2,1)S(1)}, u32[]{:S(2)}, u32[]{:S(2)}) %collective-permute-start.11) | collective-permute-done | bytes 393248 | tf_op jit(solution)/shard_map/ppermute | solution.py:17
  78.5 5.5 %collective-permute-done.12 = bf16[48,4096]{1,0:T(8,128)(2,1)S(1)} collective-permute-done((bf16[48,4096]{1,0:T(8,128)(2,1)S(1)}, bf16[48,4096]{1,0:T(8,128)(2,1)S(1)}, u32[]{:S(2)}, u32[]{:S(2)}) %collective-permute-start.12) | collective-permute-done | bytes 393248 | tf_op jit(solution)/shard_map/ppermute | solution.py:17
  87.7 10.3 %collective-permute-done.15 = bf16[48,4096]{1,0:T(8,128)(2,1)S(1)} collective-permute-done((bf16[48,4096]{1,0:T(8,128)(2,1)S(1)}, bf16[48,4096]{1,0:T(8,128)(2,1)S(1)}, u32[]{:S(2)}, u32[]{:S(2)}) %collective-permute-start.15) | collective-permute-done | bytes 393248 | tf_op jit(solution)/shard_map/ppermute | solution.py:17
  109.1 5.1 %collective-permute-done.19 = bf16[32,4096]{1,0:T(8,128)(2,1)S(1)} collective-permute-done((bf16[32,4096]{1,0:T(8,128)(2,1)}, bf16[32,4096]{1,0:T(8,128)(2,1)S(1)}, u32[]{:S(2)}, u32[]{:S(2)}) %collective-permute-start.19) | collective-permute-done | bytes 262176 | tf_op jit(solution)/shard_map/ppermute | solution.py:17
  114.2 9.9 %collective-permute-done.18 = bf16[96,4096]{1,0:T(8,128)(2,1)} collective-permute-done((bf16[96,4096]{1,0:T(8,128)(2,1)}, bf16[96,4096]{1,0:T(8,128)(2,1)}, u32[]{:S(2)}, u32[]{:S(2)}) %collective-permute-start.18) | collective-permute-done | bytes 786464 | tf_op jit(solution)/shard_map/ppermute | solution.py:17
  125.8 4.9 %project.12 = bf16[384,768]{1,0:T(8,128)(2,1)S(1)} custom-call(s32[4]{0:T(128)S(1)} %get-tuple-element.631.order_ref, s32[4]{0:T(128)S(1)} %get-tuple-element.632.places_ref, bf16[192,4096]{1,0:T(8,128)(2,1)} %pad_maximum_fusion.refs_0_, bf16[192,4096]{1,0:T(8,128)(2,1)} %collective-permute-done.20.refs_1_, ...), custom_call_target="tpu_custom_call" | custom-call | flops 1 | bytes 1 | tf_op jit(solution)/shard_map/project/pallas_call | solution.py:54
  135.7 9.5 %collective-permute-done.23 = bf16[64,4096]{1,0:T(8,128)(2,1)S(1)} collective-permute-done((bf16[64,4096]{1,0:T(8,128)(2,1)S(1)}, bf16[64,4096]{1,0:T(8,128)(2,1)S(1)}, u32[]{:S(2)}, u32[]{:S(2)}) %collective-permute-start.23) | collective-permute-done | bytes 524320 | tf_op jit(solution)/shard_map/ppermute | solution.py:17
  148.8 14.8 %collective-permute-done.24 = bf16[384,768]{1,0:T(8,128)(2,1)S(1)} collective-permute-done((bf16[384,768]{1,0:T(8,128)(2,1)S(1)}, bf16[384,768]{1,0:T(8,128)(2,1)S(1)}, u32[]{:S(2)}, u32[]{:S(2)}) %collective-permute-start.24) | collective-permute-done | bytes 589856 | tf_op jit(solution)/shard_map/ppermute | solution.py:17
  168.5 16.2 %collective-permute-done.28 = bf16[48,4096]{1,0:T(8,128)(2,1)S(1)} collective-permute-done((bf16[48,4096]{1,0:T(8,128)(2,1)S(1)}, bf16[48,4096]{1,0:T(8,128)(2,1)S(1)}, u32[]{:S(2)}, u32[]{:S(2)}) %collective-permute-start.28) | collective-permute-done | bytes 393248 | tf_op jit(solution)/shard_map/ppermute | solution.py:17
  187.7 8.3 %collective-permute-done.29 = bf16[384,768]{1,0:T(8,128)(2,1)S(1)} collective-permute-done((bf16[384,768]{1,0:T(8,128)(2,1)S(1)}, bf16[384,768]{1,0:T(8,128)(2,1)S(1)}, u32[]{:S(2)}, u32[]{:S(2)}) %collective-permute-start.29) | collective-permute-done | bytes 589856 | tf_op jit(solution)/shard_map/ppermute | solution.py:17
  201.6 12.3 %collective-permute-done.33 = bf16[48,4096]{1,0:T(8,128)(2,1)S(1)} collective-permute-done((bf16[48,4096]{1,0:T(8,128)(2,1)S(1)}, bf16[48,4096]{1,0:T(8,128)(2,1)S(1)}, u32[]{:S(2)}, u32[]{:S(2)}) %collective-permute-start.33) | collective-permute-done | bytes 393248 | tf_op jit(solution)/shard_map/ppermute | solution.py:17
  219.3 4.8 %project.15 = bf16[384,768]{1,0:T(8,128)(2,1)S(1)} custom-call(s32[4]{0:T(128)S(1)} %get-tuple-element.631.order_ref, s32[4]{0:T(128)S(1)} %get-tuple-element.632.places_ref, bf16[192,4096]{1,0:T(8,128)(2,1)} %pad_maximum_fusion.refs_0_, bf16[192,4096]{1,0:T(8,128)(2,1)} %collective-permute-done.20.refs_1_, ...), custom_call_target="tpu_custom_call" | custom-call | flops 1 | bytes 1 | tf_op jit(solution)/shard_map/project/pallas_call | solution.py:54
  230.6 7.1 %collective-permute-done.36 = bf16[96,4096]{1,0:T(8,128)(2,1)S(1)} collective-permute-done((bf16[96,4096]{1,0:T(8,128)(2,1)S(1)}, bf16[96,4096]{1,0:T(8,128)(2,1)S(1)}, u32[]{:S(2)}, u32[]{:S(2)}) %collective-permute-start.36) | collective-permute-done | bytes 786464 | tf_op jit(solution)/shard_map/ppermute | solution.py:17
  246.8 6.1 %collective-permute-done.38 = bf16[384,768]{1,0:T(8,128)(2,1)S(1)} collective-permute-done((bf16[384,768]{1,0:T(8,128)(2,1)S(1)}, bf16[384,768]{1,0:T(8,128)(2,1)S(1)}, u32[]{:S(2)}, u32[]{:S(2)}) %collective-permute-start.38) | collective-permute-done | bytes 589856 | tf_op jit(solution)/shard_map/ppermute | solution.py:17
  263.9 4.4 %collective-permute-done.40 = bf16[64,4096]{1,0:T(8,128)(2,1)S(1)} collective-permute-done((bf16[64,4096]{1,0:T(8,128)(2,1)}, bf16[64,4096]{1,0:T(8,128)(2,1)S(1)}, u32[]{:S(2)}, u32[]{:S(2)}) %collective-permute-start.40) | collective-permute-done | bytes 524320 | tf_op jit(solution)/shard_map/ppermute | solution.py:17
  268.4 4.9 %project.21 = bf16[384,768]{1,0:T(8,128)(2,1)S(1)} custom-call(s32[4]{0:T(128)S(1)} %get-tuple-element.631.order_ref, s32[4]{0:T(128)S(1)} %get-tuple-element.632.places_ref, bf16[192,4096]{1,0:T(8,128)(2,1)} %pad_maximum_fusion.3.refs_0_, bf16[192,4096]{1,0:T(8,128)(2,1)} %collective-permute-done.42.refs_1_, ...), custom_call_target="tpu_custom_call" | custom-call | flops 1 | bytes 1 | tf_op jit(solution)/shard_map/project/pallas_call | solution.py:54
  273.4 4.8 %project.20 = bf16[384,768]{1,0:T(8,128)(2,1)S(1)} custom-call(s32[4]{0:T(128)S(1)} %get-tuple-element.631.order_ref, s32[4]{0:T(128)S(1)} %get-tuple-element.632.places_ref, bf16[192,4096]{1,0:T(8,128)(2,1)} %pad_maximum_fusion.3.refs_0_, bf16[192,4096]{1,0:T(8,128)(2,1)} %collective-permute-done.42.refs_1_, ...), custom_call_target="tpu_custom_call" | custom-call | flops 1 | bytes 1 | tf_op jit(solution)/shard_map/project/pallas_call | solution.py:54
  278.2 7.5 %collective-permute-done.41 = bf16[384,768]{1,0:T(8,128)(2,1)S(1)} collective-permute-done((bf16[384,768]{1,0:T(8,128)(2,1)}, bf16[384,768]{1,0:T(8,128)(2,1)S(1)}, u32[]{:S(2)}, u32[]{:S(2)}) %collective-permute-start.41) | collective-permute-done | bytes 589856 | tf_op jit(solution)/shard_map/ppermute | solution.py:17
  287.5 3.9 collective-permute-start.47
  291.8 7.0 %collective-permute-done.47 = bf16[304,256]{1,0:T(8,128)(2,1)S(1)} collective-permute-done((bf16[304,256]{1,0:T(8,128)(2,1)S(1)}, bf16[304,256]{1,0:T(8,128)(2,1)S(1)}, u32[]{:S(2)}, u32[]{:S(2)}) %collective-permute-start.47) | collective-permute-done | bytes 155680 | tf_op jit(solution)/shard_map/ppermute | solution.py:407
  301.7 3.9 gate.2
  305.7 13.3 %collective-permute-start.49 = (bf16[512,256]{1,0:T(8,128)(2,1)S(1)}, bf16[512,256]{1,0:T(8,128)(2,1)S(1)}, u32[]{:S(2)}, u32[]{:S(2)}) collective-permute-start(bf16[512,256]{1,0:T(8,128)(2,1)S(1)} %get-tuple-element.585), channel_id=1, source_target_pairs={{0,8},{4,12},{8,0},{12,4},{16,24},{20,28},{24,16},{28,20},{1,9},{5... | collective-permute-start | bytes 786440 | tf_op jit(solution)/shard_map/ppermute | solution.py:17
  323.3 4.1 %gate.3 = bf16[2,512,256]{2,1,0:T(8,128)(2,1)S(1)} custom-call(bf16[2,144,768]{2,1,0:T(8,128)(2,1)S(1)} %pad_maximum_fusion.18.refs_0_, bf16[2,128,768]{2,1,0:T(8,128)(2,1)S(1)} %bitcast.126, bf16[2,128,768]{2,1,0:T(8,128)(2,1)S(1)} %bitcast.131, bf16[2,192,768]{2,1,0:T(8,128)(2,1)S(1)} %bitcast.120, bf16[2,192,768]{2,1,0:T(8,128)(2,1)S(1)} %bitcast.129, ...), custom_call_target="tpu_custom_call" | custom-call | flops 1 | bytes 1 | tf_op jit(solution)/shard_map/gate/pallas_call | solution.py:111
  329.8 4.2 %collective-permute-done.50 = bf16[512,256]{1,0:T(8,128)(2,1)S(1)} collective-permute-done((bf16[512,256]{1,0:T(8,128)(2,1)S(1)}, bf16[512,256]{1,0:T(8,128)(2,1)S(1)}, u32[]{:S(2)}, u32[]{:S(2)}) %collective-permute-start.50) | collective-permute-done | bytes 262176 | tf_op jit(solution)/shard_map/ppermute | solution.py:17
  334.0 4.1 %out_block.5 = bf16[512,2048]{1,0:T(8,128)(2,1)S(1)} custom-call(s32[1]{0:T(128)} %bitcast.66.block_ref, bf16[512,1024]{1,0:T(8,128)(2,1)S(1)} %maximum_dynamic-update-slice_fusion.1.gating_ref, bf16[1024,8192]{1,0:T(8,128)(2,1)} %w_ref.7), custom_call_target="tpu_custom_call" | custom-call | flops 1 | bytes 1 | tf_op jit(solution)/shard_map/out_block/pallas_call | solution.py:150
  338.2 4.1 %out_block.6 = bf16[512,2048]{1,0:T(8,128)(2,1)S(1)} custom-call(s32[1]{0:T(128)} %bitcast.39.block_ref, bf16[512,1024]{1,0:T(8,128)(2,1)S(1)} %maximum_dynamic-update-slice_fusion.1.gating_ref, bf16[1024,8192]{1,0:T(8,128)(2,1)} %w_ref.7), custom_call_target="tpu_custom_call" | custom-call | flops 1 | bytes 1 | tf_op jit(solution)/shard_map/out_block/pallas_call | solution.py:150
  342.3 4.1 %out_block.4 = bf16[512,2048]{1,0:T(8,128)(2,1)S(1)} custom-call(s32[1]{0:T(128)} %bitcast.40.block_ref, bf16[512,1024]{1,0:T(8,128)(2,1)S(1)} %maximum_dynamic-update-slice_fusion.1.gating_ref, bf16[1024,8192]{1,0:T(8,128)(2,1)} %w_ref.7), custom_call_target="tpu_custom_call" | custom-call | flops 1 | bytes 1 | tf_op jit(solution)/shard_map/out_block/pallas_call | solution.py:150
  348.7 4.1 %out_block.7 = bf16[512,2048]{1,0:T(8,128)(2,1)S(1)} custom-call(s32[1]{0:T(128)} %bitcast.block_ref, bf16[512,1024]{1,0:T(8,128)(2,1)S(1)} %maximum_dynamic-update-slice_fusion.1.gating_ref, bf16[1024,8192]{1,0:T(8,128)(2,1)} %w_ref.7), custom_call_target="tpu_custom_call" | custom-call | flops 1 | bytes 1 | tf_op jit(solution)/shard_map/out_block/pallas_call | solution.py:150
  352.8 42.6 %collective-permute-done.52 = bf16[512,2048]{1,0:T(8,128)(2,1)S(1)} collective-permute-done((bf16[512,2048]{1,0:T(8,128)(2,1)S(1)}, bf16[512,2048]{1,0:T(8,128)(2,1)S(1)}, u32[]{:S(2)}, u32[]{:S(2)}) %collective-permute-start.52) | collective-permute-done | bytes 2097184 | tf_op jit(solution)/shard_map/ppermute | solution.py:17
  (316 shorter events, 124.9 us)
Async XLA Ops:
  2.5 23.0 %collective-permute-start.2 = (bf16[48,2048]{1,0:T(8,128)(2,1)}, bf16[48,2048]{1,0:T(8,128)(2,1)}, u32[]{:S(2)}, u32[]{:S(2)}) collective-permute-start(bf16[48,2048]{1,0:T(8,128)(2,1)} %get-tuple-element.567), channel_id=1, source_target_pairs={{0,3},{1,2},{2,1},{3,0},{4,7},{5,6},{6,5},{7,4},{8,11},{9,10},{10,... | collective-permute-start | bytes 589832 | tf_op jit(solution)/shard_map/ppermute | solution.py:17
  3.4 22.1 %collective-permute-start.1 = (bf16[48,2048]{1,0:T(8,128)(2,1)}, bf16[48,2048]{1,0:T(8,128)(2,1)}, u32[]{:S(2)}, u32[]{:S(2)}) collective-permute-start(bf16[48,2048]{1,0:T(8,128)(2,1)} %get-tuple-element.568), channel_id=1, source_target_pairs={{0,2},{1,3},{2,0},{3,1},{4,6},{5,7},{6,4},{7,5},{8,10},{9,11},{10,... | collective-permute-start | bytes 589832 | tf_op jit(solution)/shard_map/ppermute | solution.py:17
  4.0 23.1 %collective-permute-start = (bf16[48,2048]{1,0:T(8,128)(2,1)}, bf16[48,2048]{1,0:T(8,128)(2,1)}, u32[]{:S(2)}, u32[]{:S(2)}) collective-permute-start(bf16[48,2048]{1,0:T(8,128)(2,1)} %get-tuple-element.569), channel_id=1, source_target_pairs={{0,1},{1,0},{2,3},{3,2},{4,5},{5,4},{6,7},{7,6},{8,9},{9,8},{10,11... | collective-permute-start | bytes 589832 | tf_op jit(solution)/shard_map/ppermute | solution.py:17
  13.6 19.8 %collective-permute-start.4 = (bf16[3,512,256]{2,1,0:T(8,128)(2,1)}, bf16[3,512,256]{2,1,0:T(8,128)(2,1)S(1)}, u32[]{:S(2)}, u32[]{:S(2)}) collective-permute-start(bf16[3,512,256]{2,1,0:T(8,128)(2,1)} %get-tuple-element.559), channel_id=1, source_target_pairs={{0,8},{4,12},{8,0},{12,4},{16,24},{20,28},{24,16},{28,20},{1,9},{5... | collective-permute-start | bytes 2359304 | tf_op jit(solution)/shard_map/ppermute | solution.py:17
  15.1 19.8 %collective-permute-start.3 = (bf16[3,512,256]{2,1,0:T(8,128)(2,1)S(1)}, bf16[3,512,256]{2,1,0:T(8,128)(2,1)S(1)}, u32[]{:S(2)}, u32[]{:S(2)}) collective-permute-start(bf16[3,512,256]{2,1,0:T(8,128)(2,1)S(1)} %get-tuple-element.520.refs_2_), channel_id=1, source_target_pairs={{0,4},{4,0},{8,12},{12,8},{16,20},{20,16},{24,28},{28,24},{1,5},{5... | collective-permute-start | bytes 2359304 | tf_op jit(solution)/shard_map/ppermute | solution.py:17
  33.4 27.2 %collective-permute-start.10 = (bf16[3,512,256]{2,1,0:T(8,128)(2,1)S(1)}, bf16[3,512,256]{2,1,0:T(8,128)(2,1)S(1)}, u32[]{:S(2)}, u32[]{:S(2)}) collective-permute-start(bf16[3,512,256]{2,1,0:T(8,128)(2,1)S(1)} %get-tuple-element.557), channel_id=1, source_target_pairs={{0,8},{4,12},{8,0},{12,4},{16,24},{20,28},{24,16},{28,20},{1,9},{5... | collective-permute-start | bytes 2359304 | tf_op jit(solution)/shard_map/ppermute | solution.py:17
  35.0 25.7 %collective-permute-start.9 = (bf16[3,512,256]{2,1,0:T(8,128)(2,1)S(1)}, bf16[3,512,256]{2,1,0:T(8,128)(2,1)S(1)}, u32[]{:S(2)}, u32[]{:S(2)}) collective-permute-start(bf16[3,512,256]{2,1,0:T(8,128)(2,1)S(1)} %get-tuple-element.521.refs_3_), channel_id=1, source_target_pairs={{0,4},{4,0},{8,12},{12,8},{16,20},{20,16},{24,28},{28,24},{1,5},{5... | collective-permute-start | bytes 2359304 | tf_op jit(solution)/shard_map/ppermute | solution.py:17
  39.5 21.2 %collective-permute-start.5 = (bf16[48,4096]{1,0:T(8,128)(2,1)S(1)}, bf16[48,4096]{1,0:T(8,128)(2,1)S(1)}, u32[]{:S(2)}, u32[]{:S(2)}) collective-permute-start(bf16[48,4096]{1,0:T(8,128)(2,1)S(1)} %pad_maximum_fusion.20), channel_id=1, source_target_pairs={{0,16},{4,20},{8,24},{12,28},{16,0},{20,4},{24,8},{28,12},{1,17},{... | collective-permute-start | bytes 1179656 | tf_op jit(solution)/shard_map/ppermute | solution.py:17
  65.3 18.6 %collective-permute-start.12 = (bf16[48,4096]{1,0:T(8,128)(2,1)S(1)}, bf16[48,4096]{1,0:T(8,128)(2,1)S(1)}, u32[]{:S(2)}, u32[]{:S(2)}) collective-permute-start(bf16[48,4096]{1,0:T(8,128)(2,1)S(1)} %pad_maximum_fusion.22), channel_id=1, source_target_pairs={{0,16},{4,20},{8,24},{12,28},{16,0},{20,4},{24,8},{28,12},{1,17},{... | collective-permute-start | bytes 1179656 | tf_op jit(solution)/shard_map/ppermute | solution.py:17
  103.9 21.8 %collective-permute-start.20 = (bf16[192,4096]{1,0:T(8,128)(2,1)}, bf16[192,4096]{1,0:T(8,128)(2,1)}, u32[]{:S(2)}, u32[]{:S(2)}) collective-permute-start(bf16[192,4096]{1,0:T(8,128)(2,1)} %pad_maximum_fusion.refs_0_), channel_id=1, source_target_pairs={{0,1},{1,0},{2,3},{3,2},{4,5},{5,4},{6,7},{7,6},{8,9},{9,8},{10,11... | collective-permute-start | bytes 4718600 | tf_op jit(solution)/shard_map/ppermute | solution.py:17
  103.9 20.3 %collective-permute-start.18 = (bf16[96,4096]{1,0:T(8,128)(2,1)}, bf16[96,4096]{1,0:T(8,128)(2,1)}, u32[]{:S(2)}, u32[]{:S(2)}) collective-permute-start(bf16[96,4096]{1,0:T(8,128)(2,1)} %pad_maximum_fusion.9), channel_id=1, source_target_pairs={{0,2},{1,3},{2,0},{3,1},{4,6},{5,7},{6,4},{7,5},{8,10},{9,11},{10,... | collective-permute-start | bytes 2359304 | tf_op jit(solution)/shard_map/ppermute | solution.py:17
  108.1 22.6 %collective-permute-start.21 = (bf16[3,512,256]{2,1,0:T(8,128)(2,1)S(1)}, bf16[3,512,256]{2,1,0:T(8,128)(2,1)S(1)}, u32[]{:S(2)}, u32[]{:S(2)}) collective-permute-start(bf16[3,512,256]{2,1,0:T(8,128)(2,1)S(1)} %get-tuple-element.556), channel_id=1, source_target_pairs={{0,8},{4,12},{8,0},{12,4},{16,24},{20,28},{24,16},{28,20},{1,9},{5... | collective-permute-start | bytes 2359304 | tf_op jit(solution)/shard_map/ppermute | solution.py:17
  108.5 22.2 %collective-permute-start.22 = (bf16[3,512,256]{2,1,0:T(8,128)(2,1)S(1)}, bf16[3,512,256]{2,1,0:T(8,128)(2,1)S(1)}, u32[]{:S(2)}, u32[]{:S(2)}) collective-permute-start(bf16[3,512,256]{2,1,0:T(8,128)(2,1)S(1)} %get-tuple-element.528.refs_2_), channel_id=1, source_target_pairs={{0,4},{4,0},{8,12},{12,8},{16,20},{20,16},{24,28},{28,24},{1,5},{5... | collective-permute-start | bytes 2359304 | tf_op jit(solution)/shard_map/ppermute | solution.py:17
  132.1 32.3 %collective-permute-start.26 = (bf16[3,512,256]{2,1,0:T(8,128)(2,1)S(1)}, bf16[3,512,256]{2,1,0:T(8,128)(2,1)S(1)}, u32[]{:S(2)}, u32[]{:S(2)}) collective-permute-start(bf16[3,512,256]{2,1,0:T(8,128)(2,1)S(1)} %get-tuple-element.554), channel_id=1, source_target_pairs={{0,8},{4,12},{8,0},{12,4},{16,24},{20,28},{24,16},{28,20},{1,9},{5... | collective-permute-start | bytes 2359304 | tf_op jit(solution)/shard_map/ppermute | solution.py:17
  133.8 30.6 %collective-permute-start.27 = (bf16[3,512,256]{2,1,0:T(8,128)(2,1)S(1)}, bf16[3,512,256]{2,1,0:T(8,128)(2,1)S(1)}, u32[]{:S(2)}, u32[]{:S(2)}) collective-permute-start(bf16[3,512,256]{2,1,0:T(8,128)(2,1)S(1)} %get-tuple-element.529.refs_3_), channel_id=1, source_target_pairs={{0,4},{4,0},{8,12},{12,8},{16,20},{20,16},{24,28},{28,24},{1,5},{5... | collective-permute-start | bytes 2359304 | tf_op jit(solution)/shard_map/ppermute | solution.py:17
  134.3 29.3 %collective-permute-start.24 = (bf16[384,768]{1,0:T(8,128)(2,1)S(1)}, bf16[384,768]{1,0:T(8,128)(2,1)S(1)}, u32[]{:S(2)}, u32[]{:S(2)}) collective-permute-start(bf16[384,768]{1,0:T(8,128)(2,1)S(1)} %project.12), channel_id=1, source_target_pairs={{0,16},{4,20},{8,24},{12,28},{16,0},{20,4},{24,8},{28,12},{1,17},{... | collective-permute-start | bytes 1769480 | tf_op jit(solution)/shard_map/ppermute | solution.py:17
  164.4 20.3 %collective-permute-start.30 = (bf16[128,4096]{1,0:T(8,128)(2,1)S(1)}, bf16[128,4096]{1,0:T(8,128)(2,1)S(1)}, u32[]{:S(2)}, u32[]{:S(2)}) collective-permute-start(bf16[128,4096]{1,0:T(8,128)(2,1)S(1)} %pad_maximum_fusion.4.refs_0_), channel_id=1, source_target_pairs={{0,1},{1,0},{2,3},{3,2},{4,5},{5,4},{6,7},{7,6},{8,9},{9,8},{10,11... | collective-permute-start | bytes 3145736 | tf_op jit(solution)/shard_map/ppermute | solution.py:17
  164.5 20.2 %collective-permute-start.28 = (bf16[48,4096]{1,0:T(8,128)(2,1)S(1)}, bf16[48,4096]{1,0:T(8,128)(2,1)S(1)}, u32[]{:S(2)}, u32[]{:S(2)}) collective-permute-start(bf16[48,4096]{1,0:T(8,128)(2,1)S(1)} %copy-done.54), channel_id=1, source_target_pairs={{0,8},{4,12},{8,0},{12,4},{16,24},{20,28},{24,16},{28,20},{1,9},{5... | collective-permute-start | bytes 1179656 | tf_op jit(solution)/shard_map/ppermute | solution.py:17
  166.9 29.2 %collective-permute-start.31 = (bf16[3,512,256]{2,1,0:T(8,128)(2,1)S(1)}, bf16[3,512,256]{2,1,0:T(8,128)(2,1)S(1)}, u32[]{:S(2)}, u32[]{:S(2)}) collective-permute-start(bf16[3,512,256]{2,1,0:T(8,128)(2,1)S(1)} %collective-permute-done.21.refs_6_), channel_id=1, source_target_pairs={{0,4},{4,0},{8,12},{12,8},{16,20},{20,16},{24,28},{28,24},{1,5},{5... | collective-permute-start | bytes 2359304 | tf_op jit(solution)/shard_map/ppermute | solution.py:17
  167.4 28.7 %collective-permute-start.29 = (bf16[384,768]{1,0:T(8,128)(2,1)S(1)}, bf16[384,768]{1,0:T(8,128)(2,1)S(1)}, u32[]{:S(2)}, u32[]{:S(2)}) collective-permute-start(bf16[384,768]{1,0:T(8,128)(2,1)S(1)} %project.13), channel_id=1, source_target_pairs={{0,16},{4,20},{8,24},{12,28},{16,0},{20,4},{24,8},{28,12},{1,17},{... | collective-permute-start | bytes 1769480 | tf_op jit(solution)/shard_map/ppermute | solution.py:17
  196.1 17.8 %collective-permute-start.33 = (bf16[48,4096]{1,0:T(8,128)(2,1)S(1)}, bf16[48,4096]{1,0:T(8,128)(2,1)S(1)}, u32[]{:S(2)}, u32[]{:S(2)}) collective-permute-start(bf16[48,4096]{1,0:T(8,128)(2,1)S(1)} %copy-done.55), channel_id=1, source_target_pairs={{0,8},{4,12},{8,0},{12,4},{16,24},{20,28},{24,16},{28,20},{1,9},{5... | collective-permute-start | bytes 1179656 | tf_op jit(solution)/shard_map/ppermute | solution.py:17
  196.2 18.6 %collective-permute-start.32 = (bf16[96,4096]{1,0:T(8,128)(2,1)S(1)}, bf16[96,4096]{1,0:T(8,128)(2,1)S(1)}, u32[]{:S(2)}, u32[]{:S(2)}) collective-permute-start(bf16[96,4096]{1,0:T(8,128)(2,1)S(1)} %pad_maximum_fusion.10), channel_id=1, source_target_pairs={{0,2},{1,3},{2,0},{3,1},{4,6},{5,7},{6,4},{7,5},{8,10},{9,11},{10,... | collective-permute-start | bytes 2359304 | tf_op jit(solution)/shard_map/ppermute | solution.py:17
  197.1 19.2 %collective-permute-start.34 = (bf16[256,768]{1,0:T(8,128)(2,1)S(1)}, bf16[256,768]{1,0:T(8,128)(2,1)S(1)}, u32[]{:S(2)}, u32[]{:S(2)}) collective-permute-start(bf16[256,768]{1,0:T(8,128)(2,1)S(1)} %project.14), channel_id=1, source_target_pairs={{0,16},{4,20},{8,24},{12,28},{16,0},{20,4},{24,8},{28,12},{1,17},{... | collective-permute-start | bytes 1179656 | tf_op jit(solution)/shard_map/ppermute | solution.py:17
  217.7 21.3 %collective-permute-start.39 = (bf16[192,4096]{1,0:T(8,128)(2,1)S(1)}, bf16[192,4096]{1,0:T(8,128)(2,1)S(1)}, u32[]{:S(2)}, u32[]{:S(2)}) collective-permute-start(bf16[192,4096]{1,0:T(8,128)(2,1)S(1)} %pad_maximum_fusion.2.refs_0_), channel_id=1, source_target_pairs={{0,1},{1,0},{2,3},{3,2},{4,5},{5,4},{6,7},{7,6},{8,9},{9,8},{10,11... | collective-permute-start | bytes 4718600 | tf_op jit(solution)/shard_map/ppermute | solution.py:17
  217.7 20.0 %collective-permute-start.36 = (bf16[96,4096]{1,0:T(8,128)(2,1)S(1)}, bf16[96,4096]{1,0:T(8,128)(2,1)S(1)}, u32[]{:S(2)}, u32[]{:S(2)}) collective-permute-start(bf16[96,4096]{1,0:T(8,128)(2,1)S(1)} %pad_maximum_fusion.11), channel_id=1, source_target_pairs={{0,2},{1,3},{2,0},{3,1},{4,6},{5,7},{6,4},{7,5},{8,10},{9,11},{10,... | collective-permute-start | bytes 2359304 | tf_op jit(solution)/shard_map/ppermute | solution.py:17
  224.1 28.8 %collective-permute-start.38 = (bf16[384,768]{1,0:T(8,128)(2,1)S(1)}, bf16[384,768]{1,0:T(8,128)(2,1)S(1)}, u32[]{:S(2)}, u32[]{:S(2)}) collective-permute-start(bf16[384,768]{1,0:T(8,128)(2,1)S(1)} %project.15), channel_id=1, source_target_pairs={{0,16},{4,20},{8,24},{12,28},{16,0},{20,4},{24,8},{28,12},{1,17},{... | collective-permute-start | bytes 1769480 | tf_op jit(solution)/shard_map/ppermute | solution.py:17
  256.1 22.2 %collective-permute-start.43 = (bf16[2,144,768]{2,1,0:T(8,128)(2,1)S(1)}, bf16[2,144,768]{2,1,0:T(8,128)(2,1)S(1)}, u32[]{:S(2)}, u32[]{:S(2)}) collective-permute-start(bf16[2,144,768]{2,1,0:T(8,128)(2,1)S(1)} %pad_maximum_fusion.15), channel_id=1, source_target_pairs={{0,4},{4,0},{8,12},{12,8},{16,20},{20,16},{24,28},{28,24},{1,5},{5... | collective-permute-start | bytes 1327112 | tf_op jit(solution)/shard_map/ppermute | solution.py:17
  257.6 28.1 %collective-permute-start.41 = (bf16[384,768]{1,0:T(8,128)(2,1)}, bf16[384,768]{1,0:T(8,128)(2,1)S(1)}, u32[]{:S(2)}, u32[]{:S(2)}) collective-permute-start(bf16[384,768]{1,0:T(8,128)(2,1)} %copy-done.48), channel_id=1, source_target_pairs={{0,16},{4,20},{8,24},{12,28},{16,0},{20,4},{24,8},{28,12},{1,17},{... | collective-permute-start | bytes 1769480 | tf_op jit(solution)/shard_map/ppermute | solution.py:17
  259.2 19.1 %collective-permute-start.44 = (bf16[2,144,768]{2,1,0:T(8,128)(2,1)S(1)}, bf16[2,144,768]{2,1,0:T(8,128)(2,1)S(1)}, u32[]{:S(2)}, u32[]{:S(2)}) collective-permute-start(bf16[2,144,768]{2,1,0:T(8,128)(2,1)S(1)} %pad_maximum_fusion.16), channel_id=1, source_target_pairs={{0,4},{4,0},{8,12},{12,8},{16,20},{20,16},{24,28},{28,24},{1,5},{5... | collective-permute-start | bytes 1327112 | tf_op jit(solution)/shard_map/ppermute | solution.py:17
  287.4 34.3 %collective-permute-start.45 = (bf16[256,768]{1,0:T(8,128)(2,1)S(1)}, bf16[256,768]{1,0:T(8,128)(2,1)S(1)}, u32[]{:S(2)}, u32[]{:S(2)}) collective-permute-start(bf16[256,768]{1,0:T(8,128)(2,1)S(1)} %project.19), channel_id=1, source_target_pairs={{0,16},{4,20},{8,24},{12,28},{16,0},{20,4},{24,8},{28,12},{1,17},{... | collective-permute-start | bytes 1179656 | tf_op jit(solution)/shard_map/ppermute | solution.py:17
  347.3 48.1 %collective-permute-start.52 = (bf16[512,2048]{1,0:T(8,128)(2,1)S(1)}, bf16[512,2048]{1,0:T(8,128)(2,1)S(1)}, u32[]{:S(2)}, u32[]{:S(2)}) collective-permute-start(bf16[512,2048]{1,0:T(8,128)(2,1)S(1)} %add_convert_fusion.1), channel_id=1, source_target_pairs={{0,2},{1,3},{2,0},{3,1},{4,6},{5,7},{6,4},{7,5},{8,10},{9,11},{10,... | collective-permute-start | bytes 6291464 | tf_op jit(solution)/shard_map/ppermute | solution.py:17
  348.5 46.9 %collective-permute-start.53 = (bf16[512,2048]{1,0:T(8,128)(2,1)S(1)}, bf16[512,2048]{1,0:T(8,128)(2,1)S(1)}, u32[]{:S(2)}, u32[]{:S(2)}) collective-permute-start(bf16[512,2048]{1,0:T(8,128)(2,1)S(1)} %out_block.6), channel_id=1, source_target_pairs={{0,1},{1,0},{2,3},{3,2},{4,5},{5,4},{6,7},{7,6},{8,9},{9,8},{10,11... | collective-permute-start | bytes 6291464 | tf_op jit(solution)/shard_map/ppermute | solution.py:17
  (85 other events, 1273.6 us)
